TPU v7x, 512 devices: a whole 4x4x16 slice. The times are simulated.
512 devices in a mesh: grp: 32 (over y, x, core), sp: 16 (over z).
Axes of the slice: x: 4, y: 4, z: 16, core: 2. Of those that a mesh axis runs over, the one named last changes fastest.
Arguments:
- hidden: bfloat16 [128, 32, 65536], P(None, 'grp', 'sp'), may hold values from -6 to 6
- queries: bfloat16 [128, 32, 32768], P(None, 'grp', 'sp'), may hold values from -210 to 210
- key_weight: bfloat16 [4096, 512], P('sp'), may hold values from -0.09375 to 0.09375
- value_weight: bfloat16 [4096, 512], P('sp'), may hold values from -0.09375 to 0.09375
- lengths: int32 [64], replicated, may hold values from 512 to 2560, as said below
- assign: int32 [64], replicated, may hold values from 0 to 31, as said below
Outputs:
- attended: bfloat16 [32, 192, 32768], P('grp', None, 'sp')
Inputs may be any that keep to these rules, and one draw needn't show every extreme that they name: Every length is a multiple of 512, and the lengths add up to 65536. `assign`: every group holds exactly two sequences, whose lengths add up to at most 3072 tokens; some group holds exactly that many.
All inputs are finite; a program needn't handle non-finite values.
Results may differ from a plain program's by a relative error of at most 0.011.
Values may be sent and summed in bfloat16 or wider, within the bound.
A program may use at most 64 MiB of HBM per device.

v0:
```python
import jax
import jax.numpy as jnp
from jax import lax
from jax.sharding import PartitionSpec as P

H = 16
KVH = 4
HD = 128


ROPE_BASE = 500000.0
NEG_FILL = -1e30


def rotate(key_sum, positions):
    head_width = key_sum.shape[-1]
    half_width = head_width // 2
    frequency = ROPE_BASE ** (-2.0 * jnp.arange(half_width, dtype=jnp.float32) / head_width)
    angles = positions.astype(jnp.float32)[:, None] * frequency[None, :]
    cosine = jnp.cos(angles)[:, None, :]
    sine_part = jnp.sin(angles)[:, None, :]
    first_half = key_sum[..., :half_width]
    second_half = key_sum[..., half_width:]
    return jnp.concatenate(
        [
            first_half * cosine - second_half * sine_part,
            second_half * cosine + first_half * sine_part,
        ],
        axis=-1,
    )


def sequence_table(lengths, assign, groups, pieces):
    counts = lengths // (groups * pieces)
    starts = jnp.cumsum(counts) - counts
    seq_ids = jnp.arange(lengths.shape[0], dtype=jnp.int32)
    earlier = (seq_ids[None, :] < seq_ids[:, None]) & (assign[None, :] == assign[:, None])
    offsets = jnp.sum(jnp.where(earlier, counts[None, :], 0), axis=1)
    return (counts, starts, offsets, seq_ids)


def kv_project(row_data, key_weight, value_weight):
    return (
        jnp.dot(
            row_data,
            lax.all_gather(key_weight, "sp", axis=0, tiled=True),
            preferred_element_type=jnp.float32,
        ),
        jnp.dot(
            row_data,
            lax.all_gather(value_weight, "sp", axis=0, tiled=True),
            preferred_element_type=jnp.float32,
        ),
    )


def finish_kv(key_sum, value_sum, positions):
    row_count = key_sum.shape[0]
    key_rows = rotate(key_sum.reshape(row_count, KVH, HD), positions).astype(jnp.bfloat16)
    values = value_sum.reshape(row_count, KVH, HD).astype(jnp.bfloat16)
    return (key_rows, values)


def per_device(hidden, queries, key_weight, value_weight, lengths, assign):
    groups = lax.axis_size("grp")
    pieces = lax.axis_size("sp")
    group_index = lax.axis_index("grp")
    piece_index = lax.axis_index("sp")
    tok_rows = hidden.shape[0]
    hidden_rows = hidden.reshape(tok_rows, -1)
    query_rows = queries.reshape(tok_rows, -1)
    capacity = 2 * (tok_rows // groups) - 2
    slot_count = capacity * groups
    counts, starts, offsets, seq_ids = sequence_table(lengths, assign, groups, pieces)
    unit_send = jnp.arange(capacity, dtype=jnp.int32)[:, None, None]
    targets = jnp.arange(groups, dtype=jnp.int32)[None, :, None]
    send_hit = (assign == targets) & (offsets <= unit_send) & (unit_send < offsets + counts)
    send_live = jnp.any(send_hit, axis=2)
    send_rows = jnp.sum(jnp.where(send_hit, starts + unit_send - offsets, 0), axis=2).reshape(-1)

    def pack(row_data):
        taken = jnp.take(row_data, send_rows, axis=0).reshape(capacity, groups, -1)
        return jnp.where(send_live[:, :, None], taken, jnp.zeros((), row_data.dtype))

    slot_ids = jnp.arange(slot_count, dtype=jnp.int32)
    unit_ids = slot_ids // groups
    lane_ids = slot_ids % groups
    recv_hit = (
        (assign[None, :] == group_index)
        & (offsets[None, :] <= unit_ids[:, None])
        & (unit_ids[:, None] < offsets[None, :] + counts[None, :])
    )
    slot_live = jnp.any(recv_hit, axis=1)
    slot_seq = jnp.where(slot_live, jnp.sum(jnp.where(recv_hit, seq_ids[None, :], 0), axis=1), -1)
    inner_pos = (
        jnp.sum(jnp.where(recv_hit, (unit_ids[:, None] - offsets[None, :]) * groups, 0), axis=1)
        + lane_ids
    )
    seq_span = jnp.sum(jnp.where(recv_hit, counts[None, :] * groups, 0), axis=1)
    arrived = (
        lax.all_to_all(pack(hidden_rows), "grp", split_axis=1, concat_axis=1, tiled=True),
        lax.all_to_all(pack(query_rows), "grp", split_axis=1, concat_axis=1, tiled=True),
    )
    slot_hidden = arrived[0].reshape(slot_count, -1)
    slot_query = arrived[1].reshape(slot_count, H, HD)
    key_sum, value_sum = kv_project(slot_hidden, key_weight, value_weight)
    slot_keys, slot_values = finish_kv(key_sum, value_sum, piece_index * seq_span + inner_pos)
    heads_here = H // pieces
    share = H // KVH
    spread_keys = jnp.repeat(slot_keys, share, axis=1)
    spread_values = jnp.repeat(slot_values, share, axis=1)
    head_query, head_keys, head_values = (
        lax.all_to_all(slot_query, "sp", split_axis=1, concat_axis=0, tiled=True),
        lax.all_to_all(spread_keys, "sp", split_axis=1, concat_axis=0, tiled=True),
        lax.all_to_all(spread_values, "sp", split_axis=1, concat_axis=0, tiled=True),
    )
    all_rows = pieces * slot_count
    per_block = 1
    while per_block < pieces and per_block * slot_count < 512 and (pieces % (2 * per_block) == 0):
        per_block = 2 * per_block
    block_rows = per_block * slot_count
    row_seq = jnp.tile(slot_seq, pieces)
    row_live = jnp.tile(slot_live, pieces)
    row_pos = (
        jnp.arange(pieces, dtype=jnp.int32)[:, None] * seq_span[None, :] + inner_pos[None, :]
    ).reshape(-1)
    score_scale = HD ** (-0.5)

    def attend(block_id):
        first_row = block_id * block_rows
        block_query = lax.dynamic_slice_in_dim(head_query, first_row, block_rows, 0)
        query_seq = lax.dynamic_slice_in_dim(row_seq, first_row, block_rows, 0)
        query_pos = lax.dynamic_slice_in_dim(row_pos, first_row, block_rows, 0)
        query_live = lax.dynamic_slice_in_dim(row_live, first_row, block_rows, 0)
        allowed = (
            (query_seq[:, None] == row_seq[None, :])
            & query_live[:, None]
            & row_live[None, :]
            & (row_pos[None, :] <= query_pos[:, None])
        )
        scores = (
            jnp.einsum("qhd,khd->hqk", block_query, head_keys, preferred_element_type=jnp.float32)
            * score_scale
        )
        scores = jnp.where(allowed[None, :, :], scores, NEG_FILL)
        row_max = jnp.max(scores, axis=2, keepdims=True)
        weights = jnp.exp(scores - row_max)
        weights = (weights / jnp.sum(weights, axis=2, keepdims=True)).astype(jnp.bfloat16)
        result = jnp.einsum(
            "hqk,khd->qhd", weights, head_values, preferred_element_type=jnp.float32
        )
        return jnp.where(query_live[:, None, None], result, 0.0).astype(jnp.bfloat16)

    attended = lax.map(attend, jnp.arange(pieces // per_block, dtype=jnp.int32)).reshape(
        all_rows, heads_here, HD
    )
    merged = lax.all_to_all(attended, "sp", split_axis=0, concat_axis=1, tiled=True)
    return merged.reshape(1, slot_count, H * HD)


def solution(mesh):
    return jax.shard_map(
        per_device,
        mesh=mesh,
        in_specs=(
            P(None, "grp", "sp"),
            P(None, "grp", "sp"),
            P("sp", None),
            P("sp", None),
            P(),
            P(),
        ),
        out_specs=P("grp", None, "sp"),
        check_vma=False,
    )
```

profile of v0, /device:TPU:6, one launch (start us, length us, event | category | flops | bytes accessed | tf_op | source)
XLA Modules:
  0.0 372.7 jit_solution(5832352490535089148)
XLA Ops:
  6.5 0.7 all-gather.3.cloned.1.call-update
  7.3 0.7 broadcast_multiply_fusion
  8.2 0.9 select_reduce_fusion.4
  9.2 0.7 iota_compare_fusion.1
  10.5 3.0 gather_fusion
  13.6 1.6 fusion.19
  15.1 10.1 %all-to-all-start = ((bf16[6,32,2048]{2,0,1:T(8,128)(2,1)}), bf16[6,32,2048]{2,0,1:T(8,128)(2,1)}, u32[]{:S(2)}, u32[]{:S(2)}) async-start(bf16[6,32,2048]{2,0,1:T(8,128)(2,1)} %fusion.19), calls=%async_computation | async-start | bytes 2097152 | tf_op jit(solution)/shard_map/all_to_all | solution.py:102
  25.3 0.7 all-gather.5.cloned.1.call-update
  26.0 1.5 gather_fusion.1
  27.5 2.5 fusion.18
  30.0 10.0 %all-to-all-done = bf16[6,32,2048]{2,0,1:T(8,128)(2,1)} async-done(((bf16[6,32,2048]{2,0,1:T(8,128)(2,1)}), bf16[6,32,2048]{2,0,1:T(8,128)(2,1)}, u32[]{:S(2)}, u32[]{:S(2)}) %all-to-all-start) | async-done | bytes 786464 | tf_op jit(solution)/shard_map/all_to_all | solution.py:102
  40.0 6.6 %all-to-all-start.2 = ((bf16[6,32,4096]{2,0,1:T(8,128)(2,1)}), bf16[6,32,4096]{2,0,1:T(8,128)(2,1)S(1)}, u32[]{:S(2)}, u32[]{:S(2)}) async-start(bf16[6,32,4096]{2,0,1:T(8,128)(2,1)} %fusion.18), calls=%async_computation.2 | async-start | bytes 4194304 | tf_op jit(solution)/shard_map/all_to_all | solution.py:101
  46.7 1.7 copy.44
  48.5 1.1 copy.45
  49.6 22.7 %all-to-all-done.2 = bf16[6,32,4096]{2,0,1:T(8,128)(2,1)S(1)} async-done(((bf16[6,32,4096]{2,0,1:T(8,128)(2,1)}), bf16[6,32,4096]{2,0,1:T(8,128)(2,1)S(1)}, u32[]{:S(2)}, u32[]{:S(2)}) %all-to-all-start.2) | async-done | bytes 1572896 | tf_op jit(solution)/shard_map/all_to_all | solution.py:101
  72.3 12.7 %all-to-all-start.1 = ((bf16[192,16,128]{2,0,1:T(8,128)(2,1)}), bf16[192,16,128]{2,0,1:T(8,128)(2,1)}, u32[]{:S(2)}, u32[]{:S(2)}) async-start(bf16[192,16,128]{2,0,1:T(8,128)(2,1)} %copy.45), calls=%async_computation.1 | async-start | bytes 1572864 | tf_op jit(solution)/shard_map/all_to_all | solution.py:113
  85.6 2.1 copy.49
  87.6 17.5 %all-gather.3.cloned.1.call-done = bf16[4096,512]{1,0:T(8,128)(2,1)} async-done(((bf16[256,512]{1,0:T(8,128)(2,1)}), bf16[4096,512]{1,0:T(8,128)(2,1)}) %all-gather.3.cloned.1.call-update) | async-done | bytes 4194320 | tf_op jit(solution)/shard_map/all_gather | solution.py:46
  105.2 6.5 %copy.50 = bf16[512,4096]{1,0:T(8,128)(2,1)} copy(bf16[512,4096]{0,1:T(8,128)(2,1)} %bitcast.92) | data formatting | bytes 8388608 | tf_op jit(solution)/shard_map/dot_general | solution.py:44
  111.7 3.7 fusion.29
  115.8 7.3 %all-to-all-done.1 = bf16[192,16,128]{2,0,1:T(8,128)(2,1)} async-done(((bf16[192,16,128]{2,0,1:T(8,128)(2,1)}), bf16[192,16,128]{2,0,1:T(8,128)(2,1)}, u32[]{:S(2)}, u32[]{:S(2)}) %all-to-all-start.1) | async-done | bytes 786464 | tf_op jit(solution)/shard_map/all_to_all | solution.py:113
  123.0 1.0 broadcast_in_dim.173
  124.1 10.0 %all-to-all-start.3 = ((bf16[192,16,128]{2,0,1:T(8,128)(2,1)}), bf16[192,16,128]{2,0,1:T(8,128)(2,1)S(1)}, u32[]{:S(2)}, u32[]{:S(2)}) async-start(bf16[192,16,128]{2,0,1:T(8,128)(2,1)} %bitcast.13), calls=%async_computation.3 | async-start | bytes 1572864 | tf_op jit(solution)/shard_map/all_to_all | solution.py:114
  134.0 85.6 %all-gather.5.cloned.1.call-done = bf16[4096,512]{1,0:T(8,128)(2,1)} async-done(((bf16[256,512]{1,0:T(8,128)(2,1)}), bf16[4096,512]{1,0:T(8,128)(2,1)}) %all-gather.5.cloned.1.call-update) | async-done | bytes 4194320 | tf_op jit(solution)/shard_map/all_gather | solution.py:51
  219.6 6.5 %copy.51 = bf16[512,4096]{1,0:T(8,128)(2,1)} copy(bf16[512,4096]{0,1:T(8,128)(2,1)} %bitcast.93) | data formatting | bytes 8388608 | tf_op jit(solution)/shard_map/dot_general | solution.py:49
  226.1 4.4 %convolution_convert_fusion = bf16[192,4,128]{2,0,1:T(8,128)(2,1)} fusion(bf16[192,4096,1]{1,0,2:T(8,128)(2,1)S(1)} %bitcast.101, bf16[4,128,4096]{2,1,0:T(8,128)(2,1)} %bitcast.94), kind=kOutput, calls=%fused_computation.23 | convolution fusion | flops 805404672 | bytes 5963776 | tf_op jit(solution)/shard_map/dot_general | solution.py:49
  230.5 2.0 broadcast_in_dim.174
  232.4 6.9 %all-to-all-start.4 = ((bf16[192,16,128]{2,0,1:T(8,128)(2,1)}), bf16[192,16,128]{2,0,1:T(8,128)(2,1)S(1)}, u32[]{:S(2)}, u32[]{:S(2)}) async-start(bf16[192,16,128]{2,0,1:T(8,128)(2,1)} %bitcast.20), calls=%async_computation.4 | async-start | bytes 1572864 | tf_op jit(solution)/shard_map/all_to_all | solution.py:115
  239.7 32.4 %all-to-all-done.4 = bf16[192,16,128]{2,0,1:T(8,128)(2,1)S(1)} async-done(((bf16[192,16,128]{2,0,1:T(8,128)(2,1)}), bf16[192,16,128]{2,0,1:T(8,128)(2,1)S(1)}, u32[]{:S(2)}, u32[]{:S(2)}) %all-to-all-start.4) | async-done | bytes 786464 | tf_op jit(solution)/shard_map/all_to_all | solution.py:115
  272.1 44.3 %while.11 = (s32[]{:T(128)}, bf16[4,768,1,128]{3,1,2,0:T(8,128)(2,1)}, s32[4]{0:T(128)S(1)}, pred[3072]{0:T(1024)(128)(4,1)S(1)}, s32[3072]{0:T(1024)S(1)}, /*in...) while((s32[]{:T(128)}, ...), condition=%wide.region_11.12_spmd.clone, body=%wide.region_8.11_spmd.clone.sunk | while | flops 1238831616 | bytes 30428328 | solution.py:154
  272.1 0.7 dynamic_slice.33
  274.0 4.6 %fusion.39 = (f32[768]{0:T(1024)S(1)}, f32[768,3072]{1,0:T(8,128)S(1)}) fusion(bf16[3072,1,128]{2,0,1:T(8,128)(2,1)S(1)} %get-tuple-element.269, bf16[3072,1,128]{2,0,1:T(8,128)(2,1)} %get-tuple-element.268, s32[]{:T(128)S(6)} %select_n.166, s32[768]{0:T(1024)S(1)} %dynamic_slice.34, s32[3072]{0:T(1024)S(1)} %le.125, pred[3072]{0:T(1024)(128)(4,1)S(1)} %and.189, ...), kind=kOutput, calls=%fused_computation.68.clone.1 | convolution fusion | flops 622853376 | bytes 10457860 | tf_op jit(solution)/shard_map/while/body/eval_jaxpr/qhd,khd->hqk/dot_general | solution.py:142
  278.6 1.4 fusion.40
  280.0 3.2 fusion.41
  283.2 0.7 dynamic_slice.33
  285.1 4.6 %fusion.39 = (f32[768]{0:T(1024)S(1)}, f32[768,3072]{1,0:T(8,128)S(1)}) fusion(bf16[3072,1,128]{2,0,1:T(8,128)(2,1)S(1)} %get-tuple-element.269, bf16[3072,1,128]{2,0,1:T(8,128)(2,1)} %get-tuple-element.268, s32[]{:T(128)S(6)} %select_n.166, s32[768]{0:T(1024)S(1)} %dynamic_slice.34, s32[3072]{0:T(1024)S(1)} %le.125, pred[3072]{0:T(1024)(128)(4,1)S(1)} %and.189, ...), kind=kOutput, calls=%fused_computation.68.clone.1 | convolution fusion | flops 622853376 | bytes 10457860 | tf_op jit(solution)/shard_map/while/body/eval_jaxpr/qhd,khd->hqk/dot_general | solution.py:142
  289.7 1.4 fusion.40
  291.1 3.2 fusion.41
  296.1 4.6 %fusion.39 = (f32[768]{0:T(1024)S(1)}, f32[768,3072]{1,0:T(8,128)S(1)}) fusion(bf16[3072,1,128]{2,0,1:T(8,128)(2,1)S(1)} %get-tuple-element.269, bf16[3072,1,128]{2,0,1:T(8,128)(2,1)} %get-tuple-element.268, s32[]{:T(128)S(6)} %select_n.166, s32[768]{0:T(1024)S(1)} %dynamic_slice.34, s32[3072]{0:T(1024)S(1)} %le.125, pred[3072]{0:T(1024)(128)(4,1)S(1)} %and.189, ...), kind=kOutput, calls=%fused_computation.68.clone.1 | convolution fusion | flops 622853376 | bytes 10457860 | tf_op jit(solution)/shard_map/while/body/eval_jaxpr/qhd,khd->hqk/dot_general | solution.py:142
  300.8 1.4 fusion.40
  302.2 3.2 fusion.41
  307.2 4.6 %fusion.39 = (f32[768]{0:T(1024)S(1)}, f32[768,3072]{1,0:T(8,128)S(1)}) fusion(bf16[3072,1,128]{2,0,1:T(8,128)(2,1)S(1)} %get-tuple-element.269, bf16[3072,1,128]{2,0,1:T(8,128)(2,1)} %get-tuple-element.268, s32[]{:T(128)S(6)} %select_n.166, s32[768]{0:T(1024)S(1)} %dynamic_slice.34, s32[3072]{0:T(1024)S(1)} %le.125, pred[3072]{0:T(1024)(128)(4,1)S(1)} %and.189, ...), kind=kOutput, calls=%fused_computation.68.clone.1 | convolution fusion | flops 622853376 | bytes 10457860 | tf_op jit(solution)/shard_map/while/body/eval_jaxpr/qhd,khd->hqk/dot_general | solution.py:142
  311.8 1.4 fusion.40
  313.2 3.2 fusion.41
  317.0 2.4 reduce.5
  319.6 43.7 %all_to_all.79 = bf16[16,2,12288]{2,1,0:T(2,128)(2,1)S(1)} all-to-all(bf16[16,2,12288]{2,1,0:T(2,128)(2,1)S(1)} %reshape.392), channel_id=1, replica_groups=mesh['grp'=32,'sp'=16] {'sp'}, dimensions={0} | all-to-all | bytes 1572864 | tf_op jit(solution)/shard_map/all_to_all | solution.py:157
  363.3 0.7 reshape.393
  364.7 1.2 reshape.370
  (84 shorter events, 7.2 us)
Async XLA Ops:
  6.5 19.5 %copy-start = (bf16[128,1,4096]{2,0,1:T(8,128)(2,1)S(1)}, bf16[128,1,4096]{2,0,1:T(8,128)(2,1)}, u32[]{:S(2)}) copy-start(bf16[128,1,4096]{2,0,1:T(8,128)(2,1)} %param.8) | copy-start | bytes 3145732
  6.5 98.6 %all-gather.3.cloned.1.call-start = ((), (), s32[]{:S(2)}) async-start(), calls=%async_computation.6 | async-start | bytes 4456448 | tf_op jit(solution)/shard_map/all_gather | solution.py:46
  15.1 24.9 %all-to-all-start = ((bf16[6,32,2048]{2,0,1:T(8,128)(2,1)}), bf16[6,32,2048]{2,0,1:T(8,128)(2,1)}, u32[]{:S(2)}, u32[]{:S(2)}) async-start(bf16[6,32,2048]{2,0,1:T(8,128)(2,1)} %fusion.19), calls=%async_computation | async-start | bytes 2097152 | tf_op jit(solution)/shard_map/all_to_all | solution.py:102
  25.3 194.4 %all-gather.5.cloned.1.call-start = ((), (), s32[]{:S(2)}) async-start(), calls=%async_computation.7 | async-start | bytes 4456448 | tf_op jit(solution)/shard_map/all_gather | solution.py:51
  40.0 32.3 %all-to-all-start.2 = ((bf16[6,32,4096]{2,0,1:T(8,128)(2,1)}), bf16[6,32,4096]{2,0,1:T(8,128)(2,1)S(1)}, u32[]{:S(2)}, u32[]{:S(2)}) async-start(bf16[6,32,4096]{2,0,1:T(8,128)(2,1)} %fusion.18), calls=%async_computation.2 | async-start | bytes 4194304 | tf_op jit(solution)/shard_map/all_to_all | solution.py:101
  46.7 38.3 %copy-start.2 = (s32[64]{0:T(128)S(1)}, s32[64]{0:T(128)}, u32[]{:S(2)}) copy-start(s32[64]{0:T(128)} %param.13) | copy-start | bytes 772
  72.3 50.7 %all-to-all-start.1 = ((bf16[192,16,128]{2,0,1:T(8,128)(2,1)}), bf16[192,16,128]{2,0,1:T(8,128)(2,1)}, u32[]{:S(2)}, u32[]{:S(2)}) async-start(bf16[192,16,128]{2,0,1:T(8,128)(2,1)} %copy.45), calls=%async_computation.1 | async-start | bytes 1572864 | tf_op jit(solution)/shard_map/all_to_all | solution.py:113
  105.2 6.5 %copy-start.1 = (bf16[6,32,4096]{2,1,0:T(8,128)(2,1)S(1)}, bf16[6,32,4096]{2,1,0:T(8,128)(2,1)}, u32[]{:S(2)}) copy-start(bf16[6,32,4096]{2,1,0:T(8,128)(2,1)} %copy.49) | copy-start | bytes 4718596
  124.1 106.4 %all-to-all-start.3 = ((bf16[192,16,128]{2,0,1:T(8,128)(2,1)}), bf16[192,16,128]{2,0,1:T(8,128)(2,1)S(1)}, u32[]{:S(2)}, u32[]{:S(2)}) async-start(bf16[192,16,128]{2,0,1:T(8,128)(2,1)} %bitcast.13), calls=%async_computation.3 | async-start | bytes 1572864 | tf_op jit(solution)/shard_map/all_to_all | solution.py:114
  232.4 39.7 %all-to-all-start.4 = ((bf16[192,16,128]{2,0,1:T(8,128)(2,1)}), bf16[192,16,128]{2,0,1:T(8,128)(2,1)S(1)}, u32[]{:S(2)}, u32[]{:S(2)}) async-start(bf16[192,16,128]{2,0,1:T(8,128)(2,1)} %bitcast.20), calls=%async_computation.4 | async-start | bytes 1572864 | tf_op jit(solution)/shard_map/all_to_all | solution.py:115
Sparse Core Ops, SparseCore 0:
  9.4 95.6 all-gather.2
  107.3 112.3 all-gather.4
where the time goes:
time: 375 us; the launch traced here: 373 us
  waiting for transfers between devices  177 us (47%)
  starting transfers between devices  46.3 us (12%)
  blocking collectives  43.7 us (12%)
  matrix products  39.4 us (11%)
  local copies, waits for them, and re-layouts  34.1 us (9%)
  other arithmetic  15.9 us (4%)
  between operations  13.7 us (4%)
    all_gather x1, waiting for transfers between devices, kv_project(): lax.all_gather(value_weight, 'sp', axis=0, tiled=True)  85.6 us
    all_to_all x1, blocking collectives, per_device(): lax.all_to_all(attended, 'sp', split_axis=0, concat_axis=1, tiled=True)  43.7 us
    all_to_all x1, waiting for transfers between devices, per_device(): lax.all_to_all(spread_values, 'sp', split_axis=1, concat_axis=0, tiled=True)  32.4 us
    all_to_all x1, waiting for transfers between devices, per_device(): lax.all_to_all(pack(hidden_rows), 'grp', split_axis=1, concat_axis=1, til...  22.7 us
    dot_general x4, matrix products, attend(): jnp.einsum('qhd,khd->hqk', block_query, head_keys, preferred_element_type...  18.5 us
    all_gather x1, waiting for transfers between devices, kv_project(): lax.all_gather(key_weight, 'sp', axis=0, tiled=True)  17.5 us
    dot_general x4, matrix products, attend(): jnp.einsum('hqk,khd->qhd', weights, head_values, preferred_element_type=j...  12.7 us
    all_to_all x1, starting transfers between devices, per_device(): lax.all_to_all(slot_query, 'sp', split_axis=1, concat_axis=0, tiled=True)  12.7 us
  transfers between devices with their start and end apart: 7, of which 6 were waited for; matrix products, arithmetic and copies ran while one was open for 11% of the time, Pallas kernels for 0%

commit v1 on v0

v1 whole, which is shorter than its diff:
```python
import functools

import jax
import jax.numpy as jnp
from jax import lax
from jax.experimental import pallas as pl
from jax.experimental.pallas import tpu as pltpu
from jax.sharding import PartitionSpec as P

H = 16
KVH = 4
SHARE = H // KVH
HD = 128
ROPE_BASE = 500000.0
NEG_FILL = -1e30
LOG2E = 1.4426950408889634
MESH = pl.DeviceIdType.MESH
VMEM_BYTES = 56 * 1024 * 1024


def sequence_table(lengths, assign, groups, pieces):
    counts = lengths // (groups * pieces)
    starts = jnp.cumsum(counts) - counts
    seq_ids = jnp.arange(lengths.shape[0], dtype=jnp.int32)
    earlier = (seq_ids[None, :] < seq_ids[:, None]) & (assign[None, :] == assign[:, None])
    offsets = jnp.sum(jnp.where(earlier, counts[None, :], 0), axis=1)
    return counts, starts, offsets, seq_ids


def project_kernel(
    hid_ref, q_ref, wk_ref, wv_ref, sel_ref, cos_ref, sin_ref,
    kv_out, q_out,
    hid, w, acc, kvp, qp, rkv, rq,
    hid_sem, za_sem, zb_sem, xy_sem, kv_send, kv_recv, q_send, q_recv,
):
    groups = 32
    pieces = 16
    g = lax.axis_index("grp")
    z = lax.axis_index("sp")
    core = lax.rem(g, 2)
    chip = g // 2
    x = lax.rem(chip, 4)
    y = chip // 4
    zq = z // 4
    zm = lax.rem(z, 4)

    barrier = pltpu.get_barrier_semaphore()

    def greet(k, carry):
        peer = lax.rem(g + k, groups)
        pl.semaphore_signal(barrier, inc=1, device_id=(peer, z), device_id_type=MESH)
        return carry

    lax.fori_loop(1, groups, greet, 0)
    for step in (1, 2, 4, 8, 12, 14, 15):
        pl.semaphore_signal(
            barrier, inc=1, device_id=(g, lax.rem(z + step, pieces)), device_id_type=MESH
        )

    mine = jnp.where(
        core == 0,
        wk_ref[pl.ds(pl.multiple_of(chip * 16, 16), 16), :],
        wv_ref[pl.ds(pl.multiple_of(chip * 16, 16), 16), :],
    )
    w[zq, zm, y, x] = mine
    hid[core] = hid_ref[...]
    pl.semaphore_wait(barrier, groups - 1 + 7)

    hid_copy = pltpu.make_async_remote_copy(
        src_ref=hid.at[core], dst_ref=hid.at[core],
        send_sem=hid_sem.at[0], recv_sem=hid_sem.at[1],
        device_id=(g + 1 - 2 * core, z), device_id_type=MESH,
    )

    za = []
    for k in range(3):
        za.append(
            pltpu.make_async_remote_copy(
                src_ref=w.at[zq, zm, y, x], dst_ref=w.at[zq, zm, y, x],
                send_sem=za_sem.at[0, k], recv_sem=za_sem.at[1, k],
                device_id=(g, lax.rem(z + 4 * (k + 1), pieces)), device_id_type=MESH,
            )
        )
        za[-1].start()
    hid_copy.start()

    half_cols = q_ref.shape[1] // 2
    rows = q_ref.shape[0]
    qp[...] = (
        jnp.dot(sel_ref[:, :rows], q_ref[:, :half_cols], preferred_element_type=jnp.float32)
        + jnp.dot(sel_ref[:, rows:], q_ref[:, half_cols:], preferred_element_type=jnp.float32)
    ).astype(qp.dtype).reshape(qp.shape)

    def q_copy(k):
        peer = lax.rem(g + k, groups)
        return pltpu.make_async_remote_copy(
            src_ref=qp.at[peer], dst_ref=rq.at[g],
            send_sem=q_send.at[k], recv_sem=q_recv.at[g],
            device_id=(peer, z), device_id_type=MESH,
        )

    def q_wait(k):
        source = lax.rem(g + groups - k, groups)
        return pltpu.make_async_remote_copy(
            src_ref=qp.at[source], dst_ref=rq.at[source],
            send_sem=q_send.at[k], recv_sem=q_recv.at[source],
            device_id=(source, z), device_id_type=MESH,
        )

    def kv_copy(k):
        peer = lax.rem(g + k, groups)
        return pltpu.make_async_remote_copy(
            src_ref=kvp.at[peer], dst_ref=rkv.at[chip, core],
            send_sem=kv_send.at[k], recv_sem=kv_recv.at[g],
            device_id=(peer, z), device_id_type=MESH,
        )

    def kv_wait(k):
        source = lax.rem(g + groups - k, groups)
        return pltpu.make_async_remote_copy(
            src_ref=kvp.at[source], dst_ref=rkv.at[source // 2, lax.rem(source, 2)],
            send_sem=kv_send.at[k], recv_sem=kv_recv.at[source],
            device_id=(source, z), device_id_type=MESH,
        )

    for k in range(3):
        za[k].wait()
    zb = []
    for k, step in enumerate((1, 15, 2)):
        zb.append(
            pltpu.make_async_remote_copy(
                src_ref=w.at[:, zm, y, x], dst_ref=w.at[:, zm, y, x],
                send_sem=zb_sem.at[0, k], recv_sem=zb_sem.at[1, k],
                device_id=(g, lax.rem(z + step, pieces)), device_id_type=MESH,
            )
        )
        zb[-1].start()
    for k in range(3):
        zb[k].wait()

    lo = pl.ds(0, 256)
    hi = pl.ds(256, 256)

    def x_peer(step):
        return (2 * (y * 4 + lax.rem(x + step, 4)) + core, z)

    def y_peer(step):
        return (2 * (lax.rem(y + step, 4) * 4 + x) + core, z)

    def exchange(phase, plans):
        def copy(number, src, device, slot):
            return pltpu.make_async_remote_copy(
                src_ref=src, dst_ref=src,
                send_sem=xy_sem.at[phase, number, 0, slot],
                recv_sem=xy_sem.at[phase, number, 1, slot],
                device_id=device, device_id_type=MESH,
            )

        first = []
        for number, (place, view, peer) in enumerate(plans):
            up = copy(number, view(slice(None), place), peer(1), 0)
            down = copy(number, view(slice(None), place), peer(3), 1)
            up.start()
            down.start()
            first.append((up, down))
        second = []
        for number, (place, view, peer) in enumerate(plans):
            up, down = first[number]
            below = lax.rem(place + 3, 4)
            above = lax.rem(place + 1, 4)
            copy(number, view(slice(None), below), peer(3), 0).wait_recv()
            relay_up = copy(number, view(slice(0, 2), below), peer(1), 2)
            relay_up.start()
            copy(number, view(slice(None), above), peer(1), 1).wait_recv()
            relay_down = copy(number, view(slice(2, 4), above), peer(3), 3)
            relay_down.start()
            second.append((relay_up, relay_down))
        for number, (place, view, peer) in enumerate(plans):
            far = lax.rem(place + 2, 4)
            copy(number, view(slice(0, 2), far), peer(3), 2).wait_recv()
            copy(number, view(slice(2, 4), far), peer(1), 3).wait_recv()
            for each in first[number] + second[number]:
                each.wait_send()

    exchange(0, [
        (x, lambda q, n: w.at[q, :, y, n, :, lo], x_peer),
        (y, lambda q, n: w.at[q, :, n, x, :, hi], y_peer),
    ])
    lax.fori_loop(1, groups, lambda k, c: (q_copy(k).start(), c)[1], 0)
    exchange(1, [
        (y, lambda q, n: w.at[q, :, n, :, :, lo], y_peer),
        (x, lambda q, n: w.at[q, :, :, n, :, hi], x_peer),
    ])
    hid_copy.wait()

    acc[...] = jnp.zeros_like(acc)

    def project(s, carry):
        block = w[s // 4, lax.rem(s, 4)].reshape(256, 512)
        cols = pl.ds(pl.multiple_of(s * 256, 256), 256)
        for lane in range(2):
            acc[lane] += jnp.dot(hid[lane, :, cols], block, preferred_element_type=jnp.float32)
        return carry

    lax.fori_loop(0, pieces, project, 0)
    sel = sel_ref[...]
    cos = cos_ref[...]
    sin = sin_ref[...]
    for b in range(KVH):
        part = acc[:, :, b * HD : (b + 1) * HD].reshape(2 * rows, HD)
        turned = (part * cos + pltpu.roll(part, HD // 2, 1) * sin).astype(jnp.bfloat16)
        kvp[:, :, b * HD : (b + 1) * HD] = (
            jnp.dot(sel, turned, preferred_element_type=jnp.float32)
            .astype(jnp.bfloat16)
            .reshape(groups, 16, HD)
        )

    lax.fori_loop(1, groups, lambda k, c: (kv_copy(k).start(), c)[1], 0)
    rkv[chip, core] = kvp[g]
    rq[g] = qp[g]

    def unpack_q(half):
        slot = lax.broadcasted_iota(jnp.int32, (192, 512), 0)
        col = lax.broadcasted_iota(jnp.int32, (192, 512), 1)
        hit = (slot == (col & 7) * 32 + (col >> 4)) & (((col >> 3) & 1) == half)
        return hit.astype(jnp.float32).astype(jnp.bfloat16)

    lax.fori_loop(1, groups, lambda k, c: (q_wait(k).wait_recv(), c)[1], 0)
    arrived = rq[...].reshape(512, 1024)
    for half in range(2):
        dense = jnp.dot(unpack_q(half), arrived, preferred_element_type=jnp.float32)
        for h in range(8):
            q_out[half * 8 + h] = dense[:, h * HD : (h + 1) * HD].astype(q_out.dtype)

    slot = lax.broadcasted_iota(jnp.int32, (192, 256), 0)
    col = lax.broadcasted_iota(jnp.int32, (192, 256), 1)
    unpack = (slot == (col & 7) * 32 + (col >> 3)).astype(jnp.float32).astype(jnp.bfloat16)
    lax.fori_loop(1, groups, lambda k, c: (kv_wait(k).wait_recv(), c)[1], 0)
    for kind in range(2):
        dense = jnp.dot(
            unpack, rkv[:, kind].reshape(256, 512), preferred_element_type=jnp.float32
        )
        for b in range(KVH):
            kv_out[b, kind] = dense[:, b * HD : (b + 1) * HD].astype(kv_out.dtype)

    def finish(k, carry):
        q_copy(k).wait_send()
        kv_copy(k).wait_send()
        return carry

    lax.fori_loop(1, groups, finish, 0)


def ring_kernel(
    q_ref, kv_ref, bias_ref, live_ref, o_ref,
    buf, top, total, acc, send_sem, recv_sem,
):
    pieces = 16
    half = pieces // 2
    g = lax.axis_index("grp")
    me = lax.axis_index("sp")
    above = lax.rem(me + 1, pieces)
    below = lax.rem(me + pieces - 1, pieces)

    barrier = pltpu.get_barrier_semaphore()
    for peer in (above, below):
        pl.semaphore_signal(barrier, inc=1, device_id=(g, peer), device_id_type=MESH)
    pl.semaphore_wait(barrier, 2)

    def copy(way, step, b, first=False):
        if way == 0:
            piece = lax.rem(me - step + pieces, pieces)
            peer = above
        else:
            piece = lax.rem(me + step, pieces)
            peer = below
        src = kv_ref.at[b] if first else buf.at[piece, b]
        return pltpu.make_async_remote_copy(
            src_ref=src, dst_ref=buf.at[piece, b],
            send_sem=send_sem.at[way, step, b], recv_sem=recv_sem.at[way, step, b],
            device_id=(g, peer), device_id_type=MESH,
        )

    def arrival(way, step, b):
        if way == 0:
            piece = lax.rem(me - step - 1 + pieces, pieces)
            peer = below
        else:
            piece = lax.rem(me + step + 1, pieces)
            peer = above
        return pltpu.make_async_remote_copy(
            src_ref=buf.at[piece, b], dst_ref=buf.at[piece, b],
            send_sem=send_sem.at[way, step, b], recv_sem=recv_sem.at[way, step, b],
            device_id=(g, peer), device_id_type=MESH,
        )

    for b in range(KVH):
        copy(0, 0, b, True).start()
        copy(1, 0, b, True).start()

    scale = HD ** -0.5 * LOG2E

    def block(b, keys, values, bias, first):
        for h in range(SHARE):
            scores = (
                lax.dot_general(
                    q_ref[b * SHARE + h], keys, (((1,), (1,)), ((), ())),
                    preferred_element_type=jnp.float32,
                )
                * scale
                + bias
            )
            high = jnp.max(scores, axis=1, keepdims=True)
            if first:
                new_top = jnp.broadcast_to(high, (192, HD))
            else:
                old_top = top[b, h]
                new_top = jnp.maximum(old_top, high)
                fade = jnp.exp2(old_top - new_top)
            weights = jnp.exp2(scores - new_top[:, :1])
            part = jnp.dot(weights.astype(jnp.bfloat16), values, preferred_element_type=jnp.float32)
            added = jnp.sum(weights, axis=1, keepdims=True)
            if first:
                total[b, h] = jnp.broadcast_to(added, (192, HD))
                acc[b, h] = part
            else:
                total[b, h] = total[b, h] * fade + added
                acc[b, h] = acc[b, h] * fade + part
            top[b, h] = new_top

    def own(b, carry):
        block(b, kv_ref[b, 0], kv_ref[b, 1], bias_ref[1], True)
        return carry

    lax.fori_loop(0, KVH, own, 0)

    def attend(piece, b):
        block(b, buf[piece, b, 0], buf[piece, b, 1], bias_ref[0], False)

    def ring(index, carry):
        step = index // KVH
        b = lax.rem(index, KVH)
        arrival(0, step, b).wait_recv()

        @pl.when((step < half - 2) | (b < KVH // 2))
        def _():
            copy(0, step + 1, b).start()

        arrival(1, step, b).wait_recv()

        @pl.when((step < half - 2) | (b >= KVH // 2))
        def _():
            copy(1, step + 1, b).start()

        @pl.when(me - step - 1 >= 0)
        def _():
            attend(me - step - 1, b)

        @pl.when(me + step + 1 >= pieces)
        def _():
            attend(me + step + 1 - pieces, b)

        return carry

    lax.fori_loop(0, (half - 1) * KVH, ring, 0)

    for b in range(KVH):
        arrival(0 if b < KVH // 2 else 1, half - 1, b).wait_recv()

        @pl.when(me >= half)
        def _():
            attend(me - half, b)

    def emit(b, carry):
        for h in range(SHARE):
            cols = pl.ds(pl.multiple_of(b * (SHARE * HD), SHARE * HD) + h * HD, HD)
            o_ref[:, cols] = jnp.where(
                live_ref[...] > 0, acc[b, h] / total[b, h], 0.0
            ).astype(o_ref.dtype)
        return carry

    lax.fori_loop(0, KVH, emit, 0)

    for b in range(KVH):
        copy(0, 0, b, True).wait_send()
        copy(1, 0, b, True).wait_send()

    def finish(index, carry):
        step = index // KVH
        b = lax.rem(index, KVH)
        copy(0, step, b).wait_send()
        copy(1, step, b).wait_send()
        return carry

    lax.fori_loop(KVH, (half - 1) * KVH, finish, 0)
    for b in range(KVH):
        copy(0 if b < KVH // 2 else 1, half - 1, b).wait_send()


def per_device(hidden, queries, key_weight, value_weight, lengths, assign):
    groups = lax.axis_size("grp")
    pieces = lax.axis_size("sp")
    group_index = lax.axis_index("grp")
    piece_index = lax.axis_index("sp")
    rows = hidden.shape[0]
    capacity = 2 * (rows // groups) - 2
    slots = capacity * groups
    counts, starts, offsets, seq_ids = sequence_table(lengths, assign, groups, pieces)

    unit_send = jnp.arange(8, dtype=jnp.int32)[None, :, None]
    targets = jnp.arange(groups, dtype=jnp.int32)[:, None, None]
    send_hit = (assign == targets) & (offsets <= unit_send) & (unit_send < offsets + counts)
    send_row = jnp.sum(jnp.where(send_hit, starts + unit_send - offsets + 1, 0), axis=2) - 1
    source = (
        jnp.arange(2, dtype=jnp.int32)[None, :, None] * rows + send_row[:, None, :]
    )
    source = jnp.where(send_row[:, None, :] >= 0, source, -1).reshape(groups * 16, 1)
    sel = (source == jnp.arange(2 * rows, dtype=jnp.int32)[None, :]).astype(jnp.bfloat16)

    row_ids = jnp.arange(rows, dtype=jnp.int32)
    row_hit = (starts[None, :] <= row_ids[:, None]) & (row_ids[:, None] < (starts + counts)[None, :])
    base = jnp.sum(
        jnp.where(
            row_hit,
            piece_index * counts[None, :] * groups + (row_ids[:, None] - starts[None, :]) * groups,
            0,
        ),
        axis=1,
    )
    lanes = 2 * (group_index // 2) + jnp.arange(2, dtype=jnp.int32)
    positions = (base[None, :] + lanes[:, None]).reshape(-1)
    frequency = ROPE_BASE ** (-2.0 * jnp.arange(HD // 2, dtype=jnp.float32) / HD)
    angles = positions.astype(jnp.float32)[:, None] * frequency[None, :]
    is_key = group_index % 2 == 0
    cos = jnp.where(is_key, jnp.cos(angles), 1.0)
    sin = jnp.where(is_key, jnp.sin(angles), 0.0)
    cos = jnp.concatenate([cos, cos], axis=1)
    sin = jnp.concatenate([-sin, sin], axis=1)

    slot_ids = jnp.arange(slots, dtype=jnp.int32)
    unit_ids = slot_ids // groups
    recv_hit = (
        (assign[None, :] == group_index)
        & (offsets[None, :] <= unit_ids[:, None])
        & (unit_ids[:, None] < offsets[None, :] + counts[None, :])
    )
    slot_live = jnp.any(recv_hit, axis=1)
    slot_seq = jnp.where(slot_live, jnp.sum(jnp.where(recv_hit, seq_ids[None, :], 0), axis=1), -1)
    same = (slot_seq[:, None] == slot_seq[None, :]) & slot_live[:, None] & slot_live[None, :]
    causal = same & (slot_ids[None, :] <= slot_ids[:, None])
    bias = jnp.where(jnp.stack([same, causal]), 0.0, NEG_FILL).astype(jnp.float32)
    live = jnp.broadcast_to(slot_live[:, None].astype(jnp.float32), (slots, HD))

    vmem = pl.BlockSpec(memory_space=pltpu.VMEM)
    bf16 = jnp.bfloat16
    dma = pltpu.SemaphoreType.DMA
    kv, q = pl.pallas_call(
        project_kernel,
        out_shape=(
            jax.ShapeDtypeStruct((KVH, 2, slots, HD), bf16),
            jax.ShapeDtypeStruct((H, slots, HD), bf16),
        ),
        in_specs=[vmem] * 7,
        out_specs=(vmem, vmem),
        scratch_shapes=[
            pltpu.VMEM((2, rows, 4096), bf16),
            pltpu.VMEM((4, 4, 4, 4, 16, 512), bf16),
            pltpu.VMEM((2, rows, 512), jnp.float32),
            pltpu.VMEM((groups, 16, 512), bf16),
            pltpu.VMEM((groups, 16, 1024), bf16),
            pltpu.VMEM((groups // 2, 2, 16, 512), bf16),
            pltpu.VMEM((groups, 16, 1024), bf16),
            dma((2,)),
            dma((2, 3)),
            dma((2, 3)),
            dma((2, 2, 2, 4)),
            dma((groups,)),
            dma((groups,)),
            dma((groups,)),
            dma((groups,)),
        ],
        compiler_params=pltpu.CompilerParams(
            collective_id=0, has_side_effects=True, vmem_limit_bytes=VMEM_BYTES
        ),
        name="project",
    )(
        hidden.reshape(rows, -1), queries.reshape(rows, -1), key_weight, value_weight, sel, cos, sin
    )

    out = pl.pallas_call(
        ring_kernel,
        out_shape=jax.ShapeDtypeStruct((slots, H * HD), bf16),
        in_specs=[vmem] * 4,
        out_specs=vmem,
        scratch_shapes=[
            pltpu.VMEM((pieces, KVH, 2, slots, HD), bf16),
            pltpu.VMEM((KVH, SHARE, slots, HD), jnp.float32),
            pltpu.VMEM((KVH, SHARE, slots, HD), jnp.float32),
            pltpu.VMEM((KVH, SHARE, slots, HD), jnp.float32),
            dma((2, pieces // 2, KVH)),
            dma((2, pieces // 2, KVH)),
        ],
        compiler_params=pltpu.CompilerParams(
            collective_id=1, has_side_effects=True, vmem_limit_bytes=VMEM_BYTES
        ),
        name="ring",
    )(q, kv, bias, live)
    return out.reshape(1, slots, H * HD)


def solution(mesh):
    return jax.shard_map(
        per_device,
        mesh=mesh,
        in_specs=(
            P(None, "grp", "sp"),
            P(None, "grp", "sp"),
            P("sp", None),
            P("sp", None),
            P(),
            P(),
        ),
        out_specs=P("grp", None, "sp"),
        check_vma=False,
    )
```

time: 375 us -> 169 us (0.45)
  waiting for transfers between devices: 177 us -> 0 us
  Pallas kernels: 0 us -> 159 us
  starting transfers between devices: 46.3 us -> 0 us
  blocking collectives: 43.7 us -> 0 us
  matrix products: 39.4 us -> 0 us
  local copies, waits for them, and re-layouts: 34.1 us -> 4.31 us
  between operations: 13.7 us -> 0.14 us
  other arithmetic: 15.9 us -> 4.75 us
    pallas_call x0 -> x2, Pallas kernels: none -> 159 us  [the longest x1 81.9 us: per_device(): pl.pallas_call(project_kernel, out_shape=(jax.ShapeDtypeStruct((KVH, 2, s...]
    all_gather x2 -> x0, waiting for transfers between devices: 103 us -> none  [the longest x1 85.6 us: kv_project(): lax.all_gather(value_weight, 'sp', axis=0, tiled=True)]
    all_to_all x5 -> x0, waiting for transfers between devices: 72.4 us -> none  [the longest x1 32.4 us: per_device(): lax.all_to_all(spread_values, 'sp', split_axis=1, concat_axis=0, tiled=True)]
    all_to_all x5 -> x0, starting transfers between devices: 46.2 us -> none  [the longest x1 12.7 us: per_device(): lax.all_to_all(slot_query, 'sp', split_axis=1, concat_axis=0, tiled=True)]
    all_to_all x1 -> x0, blocking collectives: 43.7 us -> none  [per_device(): lax.all_to_all(attended, 'sp', split_axis=0, concat_axis=1, tiled=True)]
    dot_general x10 -> x0, matrix products: 39.4 us -> none  [the longest x4 18.5 us: attend(): jnp.einsum('qhd,khd->hqk', block_query, head_keys, preferred_element_type...]
    dot_general x2 -> x0, local copies, waits for them, and re-layouts: 13 us -> none  [the longest x1 6.52 us: kv_project(): jnp.dot(row_data, lax.all_gather(key_weight, 'sp', axis=0, tiled=True), p...]
    reduce_sum x6 -> x3, other arithmetic: 5.86 us -> 0.84 us  [the longest x1 0.62 us: per_device(): jnp.sum(jnp.where(send_hit, starts + unit_send - offsets + 1, 0), axis=2)]
  transfers between devices with their start and end apart: 7 -> 0, of which waited for: 6 -> 0; matrix products, arithmetic and copies ran while one was open for 11% -> 0% of each run, Pallas kernels for 0% -> 0%
where the time goes in v1:
time: 169 us; the launch traced here: 168 us
  Pallas kernels  159 us (94%)
  other arithmetic  4.75 us (3%)
  local copies, waits for them, and re-layouts  4.31 us (3%)
    pallas_call x1, Pallas kernels, per_device(): pl.pallas_call(project_kernel, out_shape=(jax.ShapeDtypeStruct((KVH, 2, s...  81.9 us
    pallas_call x1, Pallas kernels, per_device(): pl.pallas_call(ring_kernel, out_shape=jax.ShapeDtypeStruct((slots, H * HD...  76.6 us

profile of v1, /device:TPU:6, one launch (start us, length us, event | category | flops | bytes accessed | tf_op | source)
XLA Modules:
  0.0 167.7 jit_solution(3059079049694869609)
XLA Ops:
  0.0 0.0 copy-start
  0.0 0.7 copy-done
  0.7 0.0 copy-start.1
  0.7 0.6 copy-done.1
  1.3 0.2 select_reduce_fusion.3
  1.5 0.1 copy.9
  1.6 0.1 reduce-window.8
  1.7 0.1 reduce
  1.9 0.1 select_reduce_fusion.2
  2.0 0.1 convert_bitcast_fusion
  2.0 0.1 fusion.5
  2.2 0.1 select_reduce_fusion.1
  2.3 0.6 select_reduce_fusion
  3.0 0.1 add_select_fusion.1
  3.1 0.1 select_n.86
  3.2 0.1 and_and_fusion
  3.3 0.7 broadcast_in_dim.84.live_ref
  4.0 0.8 fusion.sel_ref
  4.9 0.8 add_select_fusion.bias_ref
  5.7 0.5 fusion.4
  6.2 0.9 pad_maximum_fusion
  7.1 81.9 %project.1 = (bf16[4,2,192,128]{3,2,1,0:T(8,128)(2,1)}, bf16[16,192,128]{2,1,0:T(8,128)(2,1)}) custom-call(bf16[128,4096]{1,0:T(8,128)(2,1)} %bitcast.7, bf16[128,2048]{1,0:T(8,128)(2,1)} %bitcast.8, bf16[256,512]{1,0:T(8,128)(2,1)} %wk_ref.1, bf16[256,512]{1,0:T(8,128)(2,1)} %wv_ref.1, bf16[512,256]{1,0:T(8,128)(2,1)} %fusion.sel_ref, ...), custom_call_target="tpu_custom_call" | custom-call | tf_op jit(solution)/shard_map/project/pallas_call | solution.py:457
  89.0 76.6 %ring.1 = bf16[192,2048]{1,0:T(8,128)(2,1)} custom-call(bf16[16,192,128]{2,1,0:T(8,128)(2,1)} %get-tuple-element.7.q_ref, bf16[4,2,192,128]{3,2,1,0:T(8,128)(2,1)} %get-tuple-element.8.kv_ref, f32[2,192,192]{2,1,0:T(8,128)} %add_select_fusion.bias_ref, f32[192,128]{1,0:T(8,128)} %broadcast_in_dim.84.live_ref), custom_call_target="tpu_custom_call" | custom-call | tf_op jit(solution)/shard_map/ring/pallas_call | solution.py:490
  165.6 2.1 %copy.11 = bf16[1,192,2048]{2,1,0:T(8,128)(2,1)} copy(bf16[1,192,2048]{2,1,0:T(8,128)(2,1)} %bitcast.6) | data formatting | bytes 1572864
  (14 shorter events, 0.1 us)
Async XLA Ops:
  0.0 0.7 copy-start
  0.7 0.7 copy-start.1

commit v2 on v0

v2 whole, which is shorter than its diff:
```python
import jax
import jax.numpy as jnp
from jax import lax
from jax.experimental import pallas as pl
from jax.experimental.pallas import tpu as pltpu
from jax.sharding import PartitionSpec as P

H = 16
KVH = 4
SHARE = H // KVH
HD = 128
GROUPS = 32
PIECES = 16
ROWS = 128
SLOTS = 192
HALF = PIECES // 2
PAIR = KVH // 2
COLS = PAIR * HD
ROPE_BASE = 500000.0
NEG_FILL = -1e30
LOG2E = 1.4426950408889634
MESH = pl.DeviceIdType.MESH
VMEM_BYTES = 56 * 1024 * 1024
F32 = jnp.float32
BF16 = jnp.bfloat16


def iota(shape, dim):
    return lax.broadcasted_iota(jnp.int32, shape, dim)


def kernel(
    hid_ref, q_ref, wk_ref, wv_ref, len_row, len_col, asg_row, asg_col, freq_ref,
    o_ref, live_ref,
    hid, qin, w, acc, sel, cos, sin, kvp, qp, rkv, rq, qd, buf, bias, top, total, out_acc,
    in_sem, hid_sem, za_sem, zb_sem, xa_sem, xb_sem,
    kv_send, kv_recv, q_send, q_recv, ring_send, ring_recv,
):
    g = lax.axis_index("grp")
    z = lax.axis_index("sp")
    core = lax.rem(g, 2)
    chip = g // 2
    x = lax.rem(chip, 4)
    y = chip // 4
    zq = z // 4
    zm = lax.rem(z, 4)

    barrier = pltpu.get_barrier_semaphore()

    def greet(k, carry):
        peer = lax.rem(g + k, GROUPS)
        pl.semaphore_signal(barrier, inc=1, device_id=(peer, z), device_id_type=MESH)
        return carry

    lax.fori_loop(1, GROUPS, greet, 0)
    for step in (1, 2, 4, 8, 12, 14, 15):
        pl.semaphore_signal(
            barrier, inc=1, device_id=(g, lax.rem(z + step, PIECES)), device_id_type=MESH
        )

    hid_in = pltpu.make_async_copy(hid_ref, hid.at[core], in_sem.at[0])
    q_in = pltpu.make_async_copy(q_ref, qin, in_sem.at[1])
    hid_in.start()
    q_in.start()
    own_rows = pl.ds(pl.multiple_of(chip * 16, 16), 16)
    w[zq, zm, y, x] = jnp.where(core == 0, wk_ref[own_rows, :], wv_ref[own_rows, :])

    counts_r = (len_row[...] // (GROUPS * PIECES)).astype(F32)
    counts_c = (len_col[...] // (GROUPS * PIECES)).astype(F32)
    asg_r = asg_row[...]
    asg_c = asg_col[...]
    nseq = counts_r.shape[1]
    first = iota((nseq, nseq), 0)
    second = iota((nseq, nseq), 1)
    same_group = asg_c == asg_r
    up_c = jnp.where(first < second, counts_c, 0.0)
    up_r = jnp.where(second < first, counts_r, 0.0)
    starts_r = jnp.sum(up_c, axis=0, keepdims=True)
    starts_c = jnp.sum(up_r, axis=1, keepdims=True)
    offsets_r = jnp.sum(jnp.where(same_group, up_c, 0.0), axis=0, keepdims=True)
    offsets_c = jnp.sum(jnp.where(same_group, up_r, 0.0), axis=1, keepdims=True)

    pl.semaphore_wait(barrier, GROUPS - 1 + 7)

    def cols(half):
        return pl.ds(half * COLS, COLS)

    def rdma(src, dst, send, recv, device):
        return pltpu.make_async_remote_copy(
            src_ref=src, dst_ref=dst, send_sem=send, recv_sem=recv,
            device_id=device, device_id_type=MESH,
        )

    def za(half, k):
        part = w.at[zq, zm, y, x, :, cols(half)]
        return rdma(
            part, part, za_sem.at[half, 0, k], za_sem.at[half, 1, k],
            (g, lax.rem(z + 4 * (k + 1), PIECES)),
        )

    def zb(half, k):
        part = w.at[:, zm, y, x, :, cols(half)]
        return rdma(
            part, part, zb_sem.at[half, 0, k], zb_sem.at[half, 1, k],
            (g, lax.rem(z + (1, 15, 2)[k], PIECES)),
        )

    def x_peer(step):
        return (2 * (y * 4 + lax.rem(x + step, 4)) + core, z)

    def y_peer(step):
        return (2 * (lax.rem(y + step, 4) * 4 + x) + core, z)

    def xa(half, path, k):
        if path == 0:
            part = w.at[0:2, :, y, x, :, cols(half)]
        else:
            part = w.at[2:4, :, y, x, :, cols(half)]
        return rdma(
            part, part, xa_sem.at[half, path, 0, k], xa_sem.at[half, path, 1, k],
            (x_peer, y_peer)[path](k + 1),
        )

    def xb_view(half, path, shards, place):
        if path == 0:
            return w.at[shards, :, place, :, :, cols(half)]
        return w.at[shards, :, :, place, :, cols(half)]

    def xb(half, path, kind):
        place = (y, x)[path]
        peer = (y_peer, x_peer)[path]
        low = 2 * path
        if kind == 0:
            src, device = xb_view(half, path, slice(low, low + 2), place), peer(1)
        elif kind == 1:
            src, device = xb_view(half, path, slice(low, low + 2), place), peer(3)
        elif kind == 2:
            src, device = xb_view(half, path, slice(low, low + 1), lax.rem(place + 3, 4)), peer(1)
        else:
            src, device = (
                xb_view(half, path, slice(low + 1, low + 2), lax.rem(place + 1, 4)), peer(3)
            )
        return rdma(
            src, src, xb_sem.at[half, path, 0, kind], xb_sem.at[half, path, 1, kind], device
        )

    def xb_start(half):
        for path in range(2):
            xb(half, path, 0).start()
            xb(half, path, 1).start()

    def xb_relay(half):
        for path in range(2):
            xb(half, path, 0).wait_recv()
            xb(half, path, 2).start()
            xb(half, path, 1).wait_recv()
            xb(half, path, 3).start()

    def xb_finish(half):
        for path in range(2):
            xb(half, path, 2).wait_recv()
            xb(half, path, 3).wait_recv()

    for half in range(2):
        for k in range(3):
            za(half, k).start()
    hid_in.wait()
    hid_copy = rdma(
        hid.at[core], hid.at[core], hid_sem.at[0], hid_sem.at[1], (g + 1 - 2 * core, z)
    )
    hid_copy.start()

    row_l = iota((nseq, ROWS), 1).astype(F32)
    here = (starts_c <= row_l) & (row_l < starts_c + counts_c)
    goal = jnp.sum(
        jnp.where(here, asg_c.astype(F32) * 16.0 + offsets_c + row_l - starts_c, 0.0),
        axis=0, keepdims=True,
    ).astype(jnp.int32)
    goal = jnp.concatenate([goal, goal + 8], axis=1)
    sel[...] = (iota((GROUPS * 16, 2 * ROWS), 0) == goal).astype(F32).astype(BF16)

    def w_z():
        for half in range(2):
            for k in range(3):
                za(half, k).wait_recv()
            for k in range(3):
                zb(half, k).start()

    w_z()
    row_s = iota((ROWS, nseq), 0).astype(F32)
    here = (starts_r <= row_s) & (row_s < starts_r + counts_r)
    base = jnp.sum(
        jnp.where(
            here,
            z.astype(F32) * counts_r * GROUPS + (row_s - starts_r) * GROUPS,
            0.0,
        ),
        axis=1, keepdims=True,
    )
    is_key = core == 0
    for lane in range(2):
        angles = (base + (2 * chip + lane).astype(F32)) * freq_ref[...]
        cosine = jnp.where(is_key, jnp.cos(angles), 1.0)
        sine = jnp.where(is_key, jnp.sin(angles), 0.0)
        at = pl.ds(lane * ROWS, ROWS)
        cos[at, :] = cosine
        sin[at, :] = jnp.where(iota((ROWS, HD), 1) < HD // 2, -sine, sine)

    for k in range(3):
        zb(0, k).wait_recv()
    for path in range(2):
        for k in range(3):
            xa(0, path, k).start()

    q_in.wait()
    q_cols = H * HD // 2
    qp[...] = (
        jnp.dot(sel[:, :ROWS], qin[:, :q_cols], preferred_element_type=F32)
        + jnp.dot(sel[:, ROWS:], qin[:, q_cols:], preferred_element_type=F32)
    ).astype(BF16).reshape(qp.shape)

    for k in range(3):
        zb(1, k).wait_recv()
    for path in range(2):
        for k in range(3):
            xa(0, path, k).wait_recv()
    xb_start(0)
    xb_relay(0)
    xb_finish(0)
    for path in range(2):
        for k in range(3):
            xa(1, path, k).start()
    hid_copy.wait_recv()

    def project(half):
        acc[...] = jnp.zeros_like(acc)

        def shard(s, carry):
            block = w[s // 4, lax.rem(s, 4), :, :, :, cols(half)].reshape(256, COLS)
            part = pl.ds(pl.multiple_of(s * 256, 256), 256)
            for lane in range(2):
                acc[lane] += jnp.dot(hid[lane, :, part], block, preferred_element_type=F32)
            return carry

        lax.fori_loop(0, PIECES, shard, 0)
        for b in range(PAIR):
            at = pl.ds(b * HD, HD)
            part = acc[:, :, at].reshape(2 * ROWS, HD)
            turned = (part * cos[...] + pltpu.roll(part, HD // 2, 1) * sin[...]).astype(BF16)
            kvp[half, :, :, at] = (
                jnp.dot(sel[...], turned, preferred_element_type=F32)
                .astype(BF16)
                .reshape(GROUPS, 16, HD)
            )

    def kv_copy(half, k):
        peer = lax.rem(g + k, GROUPS)
        return rdma(
            kvp.at[half, peer], rkv.at[half, chip, core],
            kv_send.at[half, k], kv_recv.at[half, g], (peer, z),
        )

    def kv_wait(half, k):
        source = lax.rem(g + GROUPS - k, GROUPS)
        return rdma(
            kvp.at[half, source], rkv.at[half, source // 2, lax.rem(source, 2)],
            kv_send.at[half, k], kv_recv.at[half, source], (source, z),
        )

    def q_copy(k):
        peer = lax.rem(g + k, GROUPS)
        return rdma(qp.at[peer], rq.at[g], q_send.at[k], q_recv.at[g], (peer, z))

    def q_wait(k):
        source = lax.rem(g + GROUPS - k, GROUPS)
        return rdma(
            qp.at[source], rq.at[source], q_send.at[k], q_recv.at[source], (source, z)
        )

    def each_peer(act):
        def body(k, carry):
            act(k)
            return carry

        lax.fori_loop(1, GROUPS, body, 0)

    def kv_begin(half):
        each_peer(lambda k: kv_copy(half, k).start())
        rkv[half, chip, core] = kvp[half, g]

    def kv_end(half):
        slot = iota((SLOTS, 256), 0)
        col = iota((SLOTS, 256), 1)
        unpack = (slot == (col & 7) * GROUPS + (col >> 3)).astype(F32).astype(BF16)
        each_peer(lambda k: kv_wait(half, k).wait_recv())
        for kind in range(2):
            dense = jnp.dot(
                unpack, rkv[half, :, kind].reshape(256, COLS), preferred_element_type=F32
            )
            for b in range(PAIR):
                buf[z, half * PAIR + b, kind] = dense[:, b * HD : (b + 1) * HD].astype(BF16)

    above = lax.rem(z + 1, PIECES)
    below = lax.rem(z + PIECES - 1, PIECES)

    def ring_copy(way, step, b):
        if way == 0:
            piece, peer = lax.rem(z - step + PIECES, PIECES), above
        else:
            piece, peer = lax.rem(z + step, PIECES), below
        return rdma(
            buf.at[piece, b], buf.at[piece, b],
            ring_send.at[way, step, b], ring_recv.at[way, step, b], (g, peer),
        )

    def arrival(way, step, b):
        if way == 0:
            piece, peer = lax.rem(z - step - 1 + PIECES, PIECES), below
        else:
            piece, peer = lax.rem(z + step + 1, PIECES), above
        return rdma(
            buf.at[piece, b], buf.at[piece, b],
            ring_send.at[way, step, b], ring_recv.at[way, step, b], (g, peer),
        )

    def ring_begin(half):
        for b in range(half * PAIR, half * PAIR + PAIR):
            ring_copy(0, 0, b).start()
            ring_copy(1, 0, b).start()

    def relay(step, b):
        last = step >= HALF - 2
        first_head = lax.rem(b, PAIR) == 0
        arrival(0, step, b).wait_recv()

        @pl.when(jnp.logical_not(last) | first_head)
        def _():
            ring_copy(0, step + 1, b).start()

        arrival(1, step, b).wait_recv()

        @pl.when(jnp.logical_not(last) | jnp.logical_not(first_head))
        def _():
            ring_copy(1, step + 1, b).start()

    scale = HD ** -0.5 * LOG2E

    def block(piece, b, first):
        keys = buf[piece, b, 0]
        values = buf[piece, b, 1]
        mask = bias[1 if first else 0]
        for h in range(SHARE):
            scores = (
                lax.dot_general(
                    qd[b * SHARE + h], keys, (((1,), (1,)), ((), ())), preferred_element_type=F32
                )
                * scale
                + mask
            )
            high = jnp.max(scores, axis=1, keepdims=True)
            if first:
                new_top = jnp.broadcast_to(high, (SLOTS, HD))
            else:
                old_top = top[b, h]
                new_top = jnp.maximum(old_top, high)
                fade = jnp.exp2(old_top - new_top)
            weights = jnp.exp2(scores - new_top[:, :1])
            part = jnp.dot(weights.astype(BF16), values, preferred_element_type=F32)
            added = jnp.sum(weights, axis=1, keepdims=True)
            if first:
                total[b, h] = jnp.broadcast_to(added, (SLOTS, HD))
                out_acc[b, h] = part
            else:
                total[b, h] = total[b, h] * fade + added
                out_acc[b, h] = out_acc[b, h] * fade + part
            top[b, h] = new_top

    def attend(step, b):
        @pl.when(z - step - 1 >= 0)
        def _():
            block(z - step - 1, b, False)

        @pl.when(z + step + 1 >= PIECES)
        def _():
            block(z + step + 1 - PIECES, b, False)

    def heads(half, act):
        def body(b, carry):
            act(b)
            return carry

        lax.fori_loop(half * PAIR, half * PAIR + PAIR, body, 0)

    def ring_last(half):
        for b in range(half * PAIR, half * PAIR + PAIR):
            arrival(b - half * PAIR, HALF - 1, b).wait_recv()

            @pl.when(z >= HALF)
            def _():
                block(z - HALF, b, False)

    def emit(b):
        for h in range(SHARE):
            at = pl.ds(pl.multiple_of(b * (SHARE * HD), SHARE * HD) + h * HD, HD)
            o_ref[:, at] = (out_acc[b, h] / total[b, h]).astype(BF16)

    project(0)
    kv_begin(0)
    each_peer(lambda k: q_copy(k).start())
    rq[g] = qp[g]
    for path in range(2):
        for k in range(3):
            xa(1, path, k).wait_recv()
    kv_end(0)
    ring_begin(0)
    xb_start(1)

    unit_s = (iota((SLOTS, nseq), 0) >> 5).astype(F32)
    hit = (asg_r == g) & (offsets_r <= unit_s) & (unit_s < offsets_r + counts_r)
    seq_s = jnp.sum(jnp.where(hit, iota((SLOTS, nseq), 1) + 1, 0).astype(F32), axis=1, keepdims=True)
    unit_l = (iota((nseq, SLOTS), 1) >> 5).astype(F32)
    hit = (asg_c == g) & (offsets_c <= unit_l) & (unit_l < offsets_c + counts_c)
    seq_l = jnp.sum(jnp.where(hit, iota((nseq, SLOTS), 0) + 1, 0).astype(F32), axis=0, keepdims=True)
    same = (seq_s == seq_l) & (seq_s > 0.5)
    bias[0] = jnp.where(same, 0.0, NEG_FILL)
    bias[1] = jnp.where(
        same & (iota((SLOTS, SLOTS), 1) <= iota((SLOTS, SLOTS), 0)), 0.0, NEG_FILL
    )
    live_ref[...] = jnp.broadcast_to(seq_s, (SLOTS, HD))

    heads(0, lambda b: relay(0, b))
    heads(0, lambda b: relay(1, b))
    xb_relay(1)
    heads(0, lambda b: relay(2, b))

    each_peer(lambda k: q_wait(k).wait_recv())
    arrived = rq[...].reshape(GROUPS * 16, q_cols)
    slot = iota((SLOTS, GROUPS * 16), 0)
    col = iota((SLOTS, GROUPS * 16), 1)
    for part in range(2):
        unpack = (slot == (col & 7) * GROUPS + (col >> 4)) & (((col >> 3) & 1) == part)
        dense = jnp.dot(unpack.astype(F32).astype(BF16), arrived, preferred_element_type=F32)
        for h in range(H // 2):
            qd[part * (H // 2) + h] = dense[:, h * HD : (h + 1) * HD].astype(BF16)

    heads(0, lambda b: relay(3, b))
    heads(0, lambda b: block(z, b, True))

    def late(step):
        def act(b):
            relay(step, b)
            attend(step - 4, b)
            attend(step, b)

        return act

    xb_finish(1)
    project(1)
    kv_begin(1)
    heads(0, late(4))
    kv_end(1)
    ring_begin(1)
    heads(0, late(5))
    heads(1, lambda b: block(z, b, True))
    heads(0, late(6))

    def prompt(step, b):
        relay(step, b)
        attend(step, b)

    heads(1, lambda b: prompt(0, b))
    heads(0, lambda b: attend(3, b))
    heads(1, lambda b: prompt(1, b))
    ring_last(0)
    heads(0, emit)

    def steps(index, carry):
        prompt(index // PAIR, PAIR + lax.rem(index, PAIR))
        return carry

    lax.fori_loop(2 * PAIR, (HALF - 1) * PAIR, steps, 0)
    ring_last(1)
    heads(1, emit)

    hid_copy.wait_send()
    for half in range(2):
        for k in range(3):
            za(half, k).wait_send()
            zb(half, k).wait_send()
        for path in range(2):
            for k in range(3):
                xa(half, path, k).wait_send()
            for kind in range(4):
                xb(half, path, kind).wait_send()
        each_peer(lambda k: kv_copy(half, k).wait_send())
    each_peer(lambda k: q_copy(k).wait_send())

    def ring_sent(index, carry):
        ring_copy(0, index // KVH, lax.rem(index, KVH)).wait_send()
        ring_copy(1, index // KVH, lax.rem(index, KVH)).wait_send()
        return carry

    lax.fori_loop(0, (HALF - 1) * KVH, ring_sent, 0)
    for b in range(KVH):
        ring_copy(b % PAIR, HALF - 1, b).wait_send()


def per_device(hidden, queries, key_weight, value_weight, lengths, assign):
    frequency = ROPE_BASE ** (-2.0 * jnp.arange(HD // 2, dtype=F32) / HD)
    frequency = jnp.concatenate([frequency, frequency]).reshape(1, HD)
    vmem = pl.BlockSpec(memory_space=pltpu.VMEM)
    hbm = pl.BlockSpec(memory_space=pl.ANY)
    dma = pltpu.SemaphoreType.DMA
    state = pltpu.VMEM((KVH, SHARE, SLOTS, HD), F32)
    out, live = pl.pallas_call(
        kernel,
        out_shape=(
            jax.ShapeDtypeStruct((SLOTS, H * HD), BF16),
            jax.ShapeDtypeStruct((SLOTS, HD), F32),
        ),
        in_specs=[hbm, hbm] + [vmem] * 7,
        out_specs=(vmem, vmem),
        scratch_shapes=[
            pltpu.VMEM((2, ROWS, 4096), BF16),
            pltpu.VMEM((ROWS, H * HD), BF16),
            pltpu.VMEM((4, 4, 4, 4, 16, 512), BF16),
            pltpu.VMEM((2, ROWS, COLS), F32),
            pltpu.VMEM((GROUPS * 16, 2 * ROWS), BF16),
            pltpu.VMEM((2 * ROWS, HD), F32),
            pltpu.VMEM((2 * ROWS, HD), F32),
            pltpu.VMEM((2, GROUPS, 16, COLS), BF16),
            pltpu.VMEM((GROUPS, 16, H * HD // 2), BF16),
            pltpu.VMEM((2, GROUPS // 2, 2, 16, COLS), BF16),
            pltpu.VMEM((GROUPS, 16, H * HD // 2), BF16),
            pltpu.VMEM((H, SLOTS, HD), BF16),
            pltpu.VMEM((PIECES, KVH, 2, SLOTS, HD), BF16),
            pltpu.VMEM((2, SLOTS, SLOTS), F32),
            state,
            state,
            state,
            dma((2,)),
            dma((2,)),
            dma((2, 2, 3)),
            dma((2, 2, 3)),
            dma((2, 2, 2, 3)),
            dma((2, 2, 2, 4)),
            dma((2, GROUPS)),
            dma((2, GROUPS)),
            dma((GROUPS,)),
            dma((GROUPS,)),
            dma((2, HALF, KVH)),
            dma((2, HALF, KVH)),
        ],
        compiler_params=pltpu.CompilerParams(
            collective_id=0, has_side_effects=True, vmem_limit_bytes=VMEM_BYTES
        ),
        name="attend",
    )(
        hidden.reshape(ROWS, -1),
        queries.reshape(ROWS, -1),
        key_weight,
        value_weight,
        lengths.reshape(1, -1),
        lengths.reshape(-1, 1),
        assign.reshape(1, -1),
        assign.reshape(-1, 1),
        frequency,
    )
    return jnp.where(live[:, :1] > 0.5, out, jnp.zeros((), BF16))[None]


def solution(mesh):
    return jax.shard_map(
        per_device,
        mesh=mesh,
        in_specs=(
            P(None, "grp", "sp"),
            P(None, "grp", "sp"),
            P("sp", None),
            P("sp", None),
            P(),
            P(),
        ),
        out_specs=P("grp", None, "sp"),
        check_vma=False,
    )
```

time: 375 us -> 172 us (0.46)
  the two profiles are of different devices: /device:TPU:6 before, /device:TPU:16 now
where the time goes in v2:
time: 172 us
  Pallas kernels  167 us (97%)
  other arithmetic  3.8 us (2%)
    pallas_call x1, Pallas kernels, per_device(): pl.pallas_call(kernel, out_shape=(jax.ShapeDtypeStruct((SLOTS, H * HD), B...  167 us

profile of v2, /device:TPU:16, one launch (start us, length us, event | category | flops | bytes accessed | tf_op | source)
XLA Modules:
  0.0 172.1 jit_solution(15600048613005094280)
XLA Ops:
  0.0 0.0 copy-start.1
  0.0 0.6 maximum_bitcast_fusion.freq_ref
  0.7 0.0 copy-done.1
  0.7 0.0 copy-start
  0.7 0.7 copy.10.asg_col
  1.4 0.0 copy-done
  1.4 0.7 copy.9.len_col
  2.1 166.9 %attend.1 = (bf16[192,2048]{1,0:T(8,128)(2,1)}, f32[192,128]{1,0:T(8,128)}) custom-call(bf16[128,4096]{1,0:T(8,128)(2,1)} %bitcast.10, bf16[128,2048]{1,0:T(8,128)(2,1)} %bitcast.11, bf16[256,512]{1,0:T(8,128)(2,1)} %wk_ref.1, bf16[256,512]{1,0:T(8,128)(2,1)} %wv_ref.1, s32[1,64]{1,0:T(1,128)} %bitcast.12, s32[64,1]{1,0:T(8,128)} %copy.9.len_col, ...), custom_call_target="tpu_custom_call" | custom-call | tf_op jit(solution)/shard_map/attend/pallas_call | solution.py:515
  169.0 1.0 fusion
  170.0 2.1 %select_bitcast_fusion = bf16[1,192,2048]{2,1,0:T(8,128)(2,1)} fusion(bf16[192,2048]{1,0:T(8,128)(2,1)} %get-tuple-element.8, pred[192]{0:T(512)(128)(4,1)S(1)} %fusion), kind=kLoop, calls=%fused_computation | loop fusion | flops 393216 | bytes 1573056 | tf_op jit(solution)/shard_map/broadcast_in_dim | solution.py:569
  (1 shorter events, 0.0 us)
Async XLA Ops:
  0.0 0.7 copy-start.1
  0.7 0.7 copy-start

commit v3 on v2

v3 whole, which is shorter than its diff:
```python
import jax
import jax.numpy as jnp
import numpy as np
from jax import lax
from jax.experimental import pallas as pl
from jax.experimental.pallas import tpu as pltpu
from jax.sharding import PartitionSpec as P

H = 16
KVH = 4
SHARE = H // KVH
HD = 128
GROUPS = 32
PIECES = 16
ROWS = 128
SLOTS = 192
HALF = PIECES // 2
WIDE = SHARE * SLOTS
FIRST = 1
ROPE_BASE = 500000.0
NEG_FILL = -1e30
LOG2E = 1.4426950408889634
MESH = pl.DeviceIdType.MESH
VMEM_BYTES = 56 * 1024 * 1024
F32 = jnp.float32
BF16 = jnp.bfloat16


def iota(shape, dim):
    return lax.broadcasted_iota(jnp.int32, shape, dim)


def kernel(
    hid_ref, q_ref, wk_ref, wv_ref, len_ref, asg_ref, freq_ref,
    o_ref,
    hid, qin, w, sel, cos, sin, kvp, qp, rkv, rq, qd, buf, bias, live, top, total, out_acc,
    in_sem, hid_sem, wz_sem, xa_sem, xb_sem,
    kv_sem, q_sem, ring_send, ring_recv,
):
    g = lax.axis_index("grp")
    z = lax.axis_index("sp")
    core = lax.rem(g, 2)
    chip = g // 2
    x = lax.rem(chip, 4)
    y = chip // 4
    zq = z // 4
    zm = lax.rem(z, 4)

    def loop(low, high, act):
        def body(k, carry):
            act(k)
            return carry

        lax.fori_loop(low, high, body, 0)

    barrier = pltpu.get_barrier_semaphore()

    def greet(device):
        pl.semaphore_signal(barrier, inc=1, device_id=device, device_id_type=MESH)

    loop(1, PIECES, lambda k: greet((g, lax.rem(z + k, PIECES))))
    loop(1, GROUPS, lambda k: greet((lax.rem(g + k, GROUPS), z)))

    hid_in = pltpu.make_async_copy(hid_ref, hid.at[core], in_sem.at[0])
    q_in = pltpu.make_async_copy(q_ref, qin, in_sem.at[1])
    hid_in.start()
    q_in.start()
    own_rows = pl.ds(pl.multiple_of(chip * 16, 16), 16)
    w[zq, zm, y, x] = jnp.where(core == 0, wk_ref[own_rows, :], wv_ref[own_rows, :])

    nseq = len_ref.shape[1]
    first = iota((nseq, nseq), 0)
    second = iota((nseq, nseq), 1)
    diagonal = first == second
    counts_r = (len_ref[...] // (GROUPS * PIECES)).astype(F32)
    asg_r = asg_ref[...].astype(F32)
    counts_c = jnp.sum(jnp.where(diagonal, counts_r, 0.0), axis=1, keepdims=True)
    asg_c = jnp.sum(jnp.where(diagonal, asg_r, 0.0), axis=1, keepdims=True)
    same_group = asg_c == asg_r
    up_c = jnp.where(first < second, counts_c, 0.0)
    up_r = jnp.where(second < first, counts_r, 0.0)
    starts_r = jnp.sum(up_c, axis=0, keepdims=True)
    starts_c = jnp.sum(up_r, axis=1, keepdims=True)
    offsets_r = jnp.sum(jnp.where(same_group, up_c, 0.0), axis=0, keepdims=True)
    offsets_c = jnp.sum(jnp.where(same_group, up_r, 0.0), axis=1, keepdims=True)

    pl.semaphore_wait(barrier, GROUPS - 1 + PIECES - 1)

    def heads_of(part):
        return (0, FIRST) if part == 0 else (FIRST, KVH)

    def cols(part):
        low, high = heads_of(part)
        return pl.ds(low * HD, (high - low) * HD)

    def rdma(src, dst, send, recv, device):
        return pltpu.make_async_remote_copy(
            src_ref=src, dst_ref=dst, send_sem=send, recv_sem=recv,
            device_id=device, device_id_type=MESH,
        )

    def wz(part, step):
        slab = w.at[zq, zm, y, x, :, cols(part)]
        return rdma(
            slab, slab, wz_sem.at[part, 0], wz_sem.at[part, 1],
            (g, lax.rem(z + step, PIECES)),
        )

    def take(ref, sem):
        pltpu.make_async_copy(ref, ref, sem).wait()

    def wz_take(part, way):
        take(kvp.at[0 : PIECES - 1, :, cols(part)], wz_sem.at[part, way])

    def x_peer(step):
        return (2 * (y * 4 + lax.rem(x + step, 4)) + core, z)

    def y_peer(step):
        return (2 * (lax.rem(y + step, 4) * 4 + x) + core, z)

    def xa(part, path, k):
        slab = w.at[2 * path : 2 * path + 2, :, y, x, :, cols(part)]
        return rdma(
            slab, slab, xa_sem.at[part, path, 0, k], xa_sem.at[part, path, 1, k],
            (x_peer, y_peer)[path]((2, 1, 3)[k]),
        )

    def xb_view(part, path, shards, place):
        if path == 0:
            return w.at[shards, :, place, :, :, cols(part)]
        return w.at[shards, :, :, place, :, cols(part)]

    def xb(part, path, kind):
        place = (y, x)[path]
        peer = (y_peer, x_peer)[path]
        low = 2 * path
        both, one, two = slice(low, low + 2), slice(low, low + 1), slice(low + 1, low + 2)
        if part == 0:
            slab, device = xb_view(part, path, both, place), peer((2, 1, 3)[kind])
        else:
            slab, device = (
                (xb_view(part, path, one, place), peer(1)),
                (xb_view(part, path, two, place), peer(3)),
                (xb_view(part, path, two, place), peer(1)),
                (xb_view(part, path, one, place), peer(3)),
                (xb_view(part, path, one, lax.rem(place + 3, 4)), peer(1)),
                (xb_view(part, path, two, lax.rem(place + 1, 4)), peer(3)),
            )[kind]
        return rdma(
            slab, slab, xb_sem.at[part, path, 0, kind], xb_sem.at[part, path, 1, kind], device
        )

    def xb_start(kinds, part):
        for path in range(2):
            for kind in kinds:
                xb(part, path, kind).start()

    def xb_wait(kinds, part):
        for path in range(2):
            for kind in kinds:
                xb(part, path, kind).wait_recv()

    def xa_start(part):
        for path in range(2):
            for k in range(3):
                xa(part, path, k).start()

    def xa_wait(part):
        for path in range(2):
            for k in range(3):
                xa(part, path, k).wait_recv()

    for part in range(2):
        for step in (8, 7, 9, 6, 10, 5, 11, 4, 12, 3, 13, 2, 14, 1, 15):
            wz(part, step).start()
    hid_in.wait()
    hid_copy = rdma(
        hid.at[core], hid.at[core], hid_sem.at[0], hid_sem.at[1], (g + 1 - 2 * core, z)
    )
    hid_copy.start()

    row_l = iota((nseq, ROWS), 1).astype(F32)
    here = (starts_c <= row_l) & (row_l < starts_c + counts_c)
    goal = jnp.sum(
        jnp.where(here, asg_c * 16.0 + offsets_c + row_l - starts_c, 0.0), axis=0, keepdims=True
    ).astype(jnp.int32)
    goal = jnp.concatenate([goal, goal + 8], axis=1)
    sel[...] = (iota((GROUPS * 16, 2 * ROWS), 0) == goal).astype(F32).astype(BF16)

    wz_take(0, 1)
    xa_start(0)
    row_s = iota((ROWS, nseq), 0).astype(F32)
    here = (starts_r <= row_s) & (row_s < starts_r + counts_r)
    base = jnp.sum(
        jnp.where(
            here,
            z.astype(F32) * counts_r * GROUPS + (row_s - starts_r) * GROUPS,
            0.0,
        ),
        axis=1, keepdims=True,
    )
    is_key = core == 0
    for lane in range(2):
        angles = (base + (2 * chip + lane).astype(F32)) * freq_ref[...]
        cosine = jnp.where(is_key, jnp.cos(angles), 1.0)
        sine = jnp.where(is_key, jnp.sin(angles), 0.0)
        at = pl.ds(lane * ROWS, ROWS)
        cos[at, :] = cosine
        sin[at, :] = jnp.where(iota((ROWS, HD), 1) < HD // 2, -sine, sine)
    wz_take(1, 1)
    xa_wait(0)
    xb_start(range(3), 0)
    xa_start(1)

    q_in.wait()
    q_cols = H * HD // 2
    qp[...] = (
        jnp.dot(sel[:, :ROWS], qin[:, :q_cols], preferred_element_type=F32)
        + jnp.dot(sel[:, ROWS:], qin[:, q_cols:], preferred_element_type=F32)
    ).astype(BF16).reshape(qp.shape)

    def project(part):
        low, high = heads_of(part)
        wide = (high - low) * HD
        sums = sum(
            jnp.dot(
                hid[:, :, s * 1024 : (s + 1) * 1024].reshape(2 * ROWS, 1024),
                w[s, :, :, :, :, cols(part)].reshape(1024, wide),
                preferred_element_type=F32,
            )
            for s in range(4)
        )
        for b in range(low, high):
            at = pl.ds(b * HD, HD)
            rows = sums[:, (b - low) * HD : (b - low + 1) * HD]
            turned = (rows * cos[...] + pltpu.roll(rows, HD // 2, 1) * sin[...]).astype(BF16)
            kvp[:, :, at] = (
                jnp.dot(sel[...], turned, preferred_element_type=F32)
                .astype(BF16)
                .reshape(GROUPS, 16, HD)
            )

    def kv_copy(part, k):
        peer = lax.rem(g + k, GROUPS)
        return rdma(
            kvp.at[peer, :, cols(part)], rkv.at[chip, core, :, cols(part)],
            kv_sem.at[part, 0], kv_sem.at[part, 1], (peer, z),
        )

    def kv_take(part, way):
        take(kvp.at[0 : GROUPS - 1, :, cols(part)], kv_sem.at[part, way])

    def q_copy(k):
        peer = lax.rem(g + k, GROUPS)
        return rdma(qp.at[peer], rq.at[g], q_sem.at[0], q_sem.at[1], (peer, z))

    def q_take(way):
        take(qp.at[0 : GROUPS - 1], q_sem.at[way])

    def kv_begin(part):
        loop(1, GROUPS, lambda k: kv_copy(part, k).start())
        rkv[chip, core, :, cols(part)] = kvp[g, :, cols(part)]

    def kv_end(part):
        low, high = heads_of(part)
        slot = iota((SLOTS, 256), 0)
        col = iota((SLOTS, 256), 1)
        unpack = (slot == (col & 7) * GROUPS + (col >> 3)).astype(F32).astype(BF16)
        kv_take(part, 1)
        for kind in range(2):
            dense = jnp.dot(
                unpack,
                rkv[:, kind, :, cols(part)].reshape(256, (high - low) * HD),
                preferred_element_type=F32,
            )
            for b in range(low, high):
                buf[z, b, kind] = dense[:, (b - low) * HD : (b - low + 1) * HD].astype(BF16)

    above = lax.rem(z + 1, PIECES)
    below = lax.rem(z + PIECES - 1, PIECES)

    def ring_copy(way, step, b):
        if way == 0:
            piece, peer = lax.rem(z - step + PIECES, PIECES), above
        else:
            piece, peer = lax.rem(z + step, PIECES), below
        return rdma(
            buf.at[piece, b], buf.at[piece, b],
            ring_send.at[way, step, b], ring_recv.at[way, step, b], (g, peer),
        )

    def arrival(way, step, b):
        if way == 0:
            piece, peer = lax.rem(z - step - 1 + PIECES, PIECES), below
        else:
            piece, peer = lax.rem(z + step + 1, PIECES), above
        return rdma(
            buf.at[piece, b], buf.at[piece, b],
            ring_send.at[way, step, b], ring_recv.at[way, step, b], (g, peer),
        )

    def ring_begin(part):
        for b in range(*heads_of(part)):
            ring_copy(0, 0, b).start()
            ring_copy(1, 0, b).start()

    def relay(step, b):
        on = step < HALF - 2
        arrival(0, step, b).wait_recv()

        @pl.when(on | (lax.rem(b, 2) == 0))
        def _():
            ring_copy(0, step + 1, b).start()

        arrival(1, step, b).wait_recv()

        @pl.when(on | (lax.rem(b, 2) == 1))
        def _():
            ring_copy(1, step + 1, b).start()

    scale = HD ** -0.5 * LOG2E

    def block(pieces, b, mask):
        queries = qd[b]
        scores = [
            lax.dot_general(
                buf[piece, b, 0], queries, (((1,), (1,)), ((), ())), preferred_element_type=F32
            )
            * scale
            + bias[mask]
            for piece in pieces
        ]
        high = jnp.max(scores[0], axis=0, keepdims=True)
        for each in scores[1:]:
            high = jnp.maximum(high, jnp.max(each, axis=0, keepdims=True))
        if mask == 0:
            old = top[b, 0:1]
            high = jnp.maximum(old, high)
            fade = jnp.exp2(old - high)
        weights = [jnp.exp2(each - high) for each in scores]
        added = sum(jnp.sum(each, axis=0, keepdims=True) for each in weights)
        part = sum(
            lax.dot_general(
                buf[piece, b, 1], each.astype(BF16), (((0,), (0,)), ((), ())),
                preferred_element_type=F32,
            )
            for piece, each in zip(pieces, weights)
        )
        top[b, 0:1] = high
        if mask == 0:
            total[b, 0:1] = total[b, 0:1] * fade + added
            out_acc[b] = out_acc[b] * fade + part
        else:
            total[b, 0:1] = added
            out_acc[b] = part

    def attend(step, b):
        lower = z - step - 1
        upper = z + step + 1 - PIECES

        @pl.when(upper >= 0)
        def _():
            block((lower, upper), b, 0)

        @pl.when((upper < 0) & (lower >= 0))
        def _():
            block((lower,), b, 0)

    def attend_last(b):
        @pl.when(z >= HALF)
        def _():
            block((z - HALF,), b, 0)

    def emit(b):
        rows = jnp.transpose(out_acc[b] / total[b, 0:1])
        for h in range(SHARE):
            at = pl.ds(pl.multiple_of(b * (SHARE * HD), SHARE * HD) + h * HD, HD)
            o_ref[:, at] = jnp.where(
                live[...] > 0.5, rows[h * SLOTS : (h + 1) * SLOTS], 0.0
            ).astype(BF16)

    xa_wait(1)
    xb_wait(range(3), 0)
    xb_start(range(4), 1)
    hid_copy.wait_recv()
    project(0)
    kv_begin(0)
    for path in range(2):
        xb(1, path, 0).wait_recv()
        xb(1, path, 4).start()
        xb(1, path, 1).wait_recv()
        xb(1, path, 5).start()
    kv_end(0)
    ring_begin(0)
    relay(0, 0)

    unit_s = (iota((SLOTS, nseq), 0) >> 5).astype(F32)
    group = g.astype(F32)
    hit = (asg_r == group) & (offsets_r <= unit_s) & (unit_s < offsets_r + counts_r)
    seq_s = jnp.sum(
        jnp.where(hit, iota((SLOTS, nseq), 1) + 1, 0).astype(F32), axis=1, keepdims=True
    )

    def lane_slot(shape):
        lane = iota(shape, 1)
        for _ in range(SHARE - 1):
            lane = jnp.where(lane >= SLOTS, lane - SLOTS, lane)
        return lane

    unit_l = (lane_slot((nseq, WIDE)) >> 5).astype(F32)
    hit = (asg_c == group) & (offsets_c <= unit_l) & (unit_l < offsets_c + counts_c)
    seq_l = jnp.sum(
        jnp.where(hit, iota((nseq, WIDE), 0) + 1, 0).astype(F32), axis=0, keepdims=True
    )
    same = (seq_s == seq_l) & (seq_s > 0.5)
    bias[0] = jnp.where(same, 0.0, NEG_FILL)
    bias[1] = jnp.where(
        same & (iota((SLOTS, WIDE), 0) <= lane_slot((SLOTS, WIDE))), 0.0, NEG_FILL
    )
    live[...] = jnp.broadcast_to(seq_s, (SLOTS, HD))

    relay(1, 0)
    relay(2, 0)
    xb_wait(range(2, 6), 1)
    project(1)
    kv_begin(1)
    relay(3, 0)
    relay(4, 0)
    kv_end(1)
    ring_begin(1)
    loop(1, GROUPS, lambda k: q_copy(k).start())
    rq[g] = qp[g]
    relay(5, 0)
    relay(6, 0)
    loop(FIRST, KVH, lambda b: relay(0, b))
    arrival(0, HALF - 1, 0).wait_recv()
    loop(FIRST, KVH, lambda b: relay(1, b))
    q_take(1)
    arrived = rq[...].reshape(GROUPS * 16, q_cols)
    slot = iota((SLOTS, GROUPS * 16), 0)
    col = iota((SLOTS, GROUPS * 16), 1)
    for half in range(2):
        unpack = (slot == (col & 7) * GROUPS + (col >> 4)) & (((col >> 3) & 1) == half)
        dense = jnp.dot(unpack.astype(F32).astype(BF16), arrived, preferred_element_type=F32)
        for h in range(H // 2):
            head = half * (H // 2) + h
            qd[head // SHARE, pl.ds((head % SHARE) * SLOTS, SLOTS)] = dense[
                :, h * HD : (h + 1) * HD
            ].astype(BF16)

    loop(0, KVH, lambda b: block((z,), b, 1))

    rest = KVH - FIRST

    def steps(index):
        step = index // rest
        b = FIRST + lax.rem(index, rest)
        relay(step, b)
        attend(step - 2, b)

        @pl.when(b == FIRST)
        def _():
            attend(step, 0)

    loop(2 * rest, (HALF - 1) * rest, steps)
    loop(0, 2, lambda step: attend(step, 0))
    attend_last(0)
    emit(0)
    loop(FIRST, KVH, lambda b: attend(HALF - 3, b))
    loop(FIRST, KVH, lambda b: attend(HALF - 2, b))
    for b in range(FIRST, KVH):
        arrival(b % 2, HALF - 1, b).wait_recv()
        attend_last(b)
    loop(FIRST, KVH, emit)

    hid_copy.wait_send()
    for part in range(2):
        wz_take(part, 0)
        for path in range(2):
            for k in range(3):
                xa(part, path, k).wait_send()
            for kind in range(3 if part == 0 else 6):
                xb(part, path, kind).wait_send()
        kv_take(part, 0)
    q_take(0)

    def ring_sent(index):
        ring_copy(0, index // KVH, lax.rem(index, KVH)).wait_send()
        ring_copy(1, index // KVH, lax.rem(index, KVH)).wait_send()

    loop(0, (HALF - 1) * KVH, ring_sent)
    for b in range(KVH):
        ring_copy(b % 2, HALF - 1, b).wait_send()


def per_device(hidden, queries, key_weight, value_weight, lengths, assign):
    frequency = ROPE_BASE ** (-2.0 * np.arange(HD // 2) / HD)
    frequency = jnp.asarray(np.concatenate([frequency, frequency])[None], F32)
    vmem = pl.BlockSpec(memory_space=pltpu.VMEM)
    hbm = pl.BlockSpec(memory_space=pl.ANY)
    dma = pltpu.SemaphoreType.DMA
    out = pl.pallas_call(
        kernel,
        out_shape=jax.ShapeDtypeStruct((SLOTS, H * HD), BF16),
        in_specs=[hbm, hbm] + [vmem] * 5,
        out_specs=vmem,
        scratch_shapes=[
            pltpu.VMEM((2, ROWS, 4096), BF16),
            pltpu.VMEM((ROWS, H * HD), BF16),
            pltpu.VMEM((4, 4, 4, 4, 16, 512), BF16),
            pltpu.VMEM((GROUPS * 16, 2 * ROWS), BF16),
            pltpu.VMEM((2 * ROWS, HD), F32),
            pltpu.VMEM((2 * ROWS, HD), F32),
            pltpu.VMEM((GROUPS, 16, 512), BF16),
            pltpu.VMEM((GROUPS, 16, H * HD // 2), BF16),
            pltpu.VMEM((GROUPS // 2, 2, 16, 512), BF16),
            pltpu.VMEM((GROUPS, 16, H * HD // 2), BF16),
            pltpu.VMEM((KVH, WIDE, HD), BF16),
            pltpu.VMEM((PIECES, KVH, 2, SLOTS, HD), BF16),
            pltpu.VMEM((2, SLOTS, WIDE), F32),
            pltpu.VMEM((SLOTS, HD), F32),
            pltpu.VMEM((KVH, 8, WIDE), F32),
            pltpu.VMEM((KVH, 8, WIDE), F32),
            pltpu.VMEM((KVH, HD, WIDE), F32),
            dma((2,)),
            dma((2,)),
            dma((2, 2)),
            dma((2, 2, 2, 3)),
            dma((2, 2, 2, 6)),
            dma((2, 2)),
            dma((2,)),
            dma((2, HALF, KVH)),
            dma((2, HALF, KVH)),
        ],
        compiler_params=pltpu.CompilerParams(
            collective_id=0, has_side_effects=True, vmem_limit_bytes=VMEM_BYTES
        ),
        name="attend",
    )(
        hidden.reshape(ROWS, -1),
        queries.reshape(ROWS, -1),
        key_weight,
        value_weight,
        lengths.reshape(1, -1),
        assign.reshape(1, -1),
        frequency,
    )
    return out.reshape(1, SLOTS, H * HD)


def solution(mesh):
    return jax.shard_map(
        per_device,
        mesh=mesh,
        in_specs=(
            P(None, "grp", "sp"),
            P(None, "grp", "sp"),
            P("sp", None),
            P("sp", None),
            P(),
            P(),
        ),
        out_specs=P("grp", None, "sp"),
        check_vma=False,
    )
```

time: 172 us -> 140 us (0.81)
  the two profiles are of different devices: /device:TPU:16 before, /device:TPU:6 now
where the time goes in v3:
time: 140 us; the launch traced here: 139 us
  Pallas kernels  137 us (98%)
  local copies, waits for them, and re-layouts  2.09 us (1%)
    pallas_call x1, Pallas kernels, per_device(): pl.pallas_call(kernel, out_shape=jax.ShapeDtypeStruct((SLOTS, H * HD), BF...  137 us

profile of v3, /device:TPU:6, one launch (start us, length us, event | category | flops | bytes accessed | tf_op | source)
XLA Modules:
  0.0 139.1 jit_solution(10205034291262068071)
XLA Ops:
  0.0 137.0 %attend.1 = bf16[192,2048]{1,0:T(8,128)(2,1)} custom-call(bf16[128,4096]{1,0:T(8,128)(2,1)} %bitcast.6, bf16[128,2048]{1,0:T(8,128)(2,1)} %bitcast.7, bf16[256,512]{1,0:T(8,128)(2,1)} %wk_ref.1, bf16[256,512]{1,0:T(8,128)(2,1)} %wv_ref.1, s32[1,64]{1,0:T(1,128)} %bitcast.8, s32[1,64]{1,0:T(1,128)} %bitcast.9, f32[1,128]{1,0:T(1,128)} %constant.2.clone.freq_ref), custom_call_target="tpu_custom_call" | custom-call | tf_op jit(solution)/shard_map/attend/pallas_call | solution.py:502
  137.0 2.1 %copy.9 = bf16[1,192,2048]{2,1,0:T(8,128)(2,1)} copy(bf16[1,192,2048]{2,1,0:T(8,128)(2,1)} %bitcast.5) | data formatting | bytes 1572864

commit v4 on v3

--- a/solution.py
+++ b/solution.py
@@ -16,7 +16,7 @@
 SLOTS = 192
 HALF = PIECES // 2
 WIDE = SHARE * SLOTS
-FIRST = 1
+FIRST = 2
 ROPE_BASE = 500000.0
 NEG_FILL = -1e30
 LOG2E = 1.4426950408889634
@@ -34,7 +34,7 @@
     hid_ref, q_ref, wk_ref, wv_ref, len_ref, asg_ref, freq_ref,
     o_ref,
     hid, qin, w, sel, cos, sin, kvp, qp, rkv, rq, qd, buf, bias, live, top, total, out_acc,
-    in_sem, hid_sem, wz_sem, xa_sem, xb_sem,
+    in_sem, hid_sem, wz_sem, xa_send, xa_sem, xb_send, xb_sem,
     kv_sem, q_sem, ring_send, ring_recv,
 ):
     g = lax.axis_index("grp")
@@ -121,7 +121,7 @@
     def xa(part, path, k):
         slab = w.at[2 * path : 2 * path + 2, :, y, x, :, cols(part)]
         return rdma(
-            slab, slab, xa_sem.at[part, path, 0, k], xa_sem.at[part, path, 1, k],
+            slab, slab, xa_send.at[part], xa_sem.at[part, path, k],
             (x_peer, y_peer)[path]((2, 1, 3)[k]),
         )
 
@@ -147,7 +147,7 @@
                 (xb_view(part, path, two, lax.rem(place + 1, 4)), peer(3)),
             )[kind]
         return rdma(
-            slab, slab, xb_sem.at[part, path, 0, kind], xb_sem.at[part, path, 1, kind], device
+            slab, slab, xb_send.at[part], xb_sem.at[part, path, kind], device
         )
 
     def xb_start(kinds, part):
@@ -279,44 +279,48 @@
     above = lax.rem(z + 1, PIECES)
     below = lax.rem(z + PIECES - 1, PIECES)
 
-    def ring_copy(way, step, b):
+    def ring_copy(way, step, b, kind):
         if way == 0:
             piece, peer = lax.rem(z - step + PIECES, PIECES), above
         else:
             piece, peer = lax.rem(z + step, PIECES), below
         return rdma(
-            buf.at[piece, b], buf.at[piece, b],
-            ring_send.at[way, step, b], ring_recv.at[way, step, b], (g, peer),
-        )
-
-    def arrival(way, step, b):
+            buf.at[piece, b, kind], buf.at[piece, b, kind],
+            ring_send.at[way], ring_recv.at[way, step, b, kind], (g, peer),
+        )
+
+    def arrival(way, step, b, kind):
         if way == 0:
             piece, peer = lax.rem(z - step - 1 + PIECES, PIECES), below
         else:
             piece, peer = lax.rem(z + step + 1, PIECES), above
         return rdma(
-            buf.at[piece, b], buf.at[piece, b],
-            ring_send.at[way, step, b], ring_recv.at[way, step, b], (g, peer),
+            buf.at[piece, b, kind], buf.at[piece, b, kind],
+            ring_send.at[way], ring_recv.at[way, step, b, kind], (g, peer),
         )
 
     def ring_begin(part):
         for b in range(*heads_of(part)):
-            ring_copy(0, 0, b).start()
-            ring_copy(1, 0, b).start()
+            for kind in range(2):
+                ring_copy(0, 0, b, kind).start()
+                ring_copy(1, 0, b, kind).start()
 
     def relay(step, b):
         on = step < HALF - 2
-        arrival(0, step, b).wait_recv()
-
-        @pl.when(on | (lax.rem(b, 2) == 0))
-        def _():
-            ring_copy(0, step + 1, b).start()
-
-        arrival(1, step, b).wait_recv()
-
-        @pl.when(on | (lax.rem(b, 2) == 1))
-        def _():
-            ring_copy(1, step + 1, b).start()
+        for kind in range(2):
+            for way in range(2):
+                arrival(way, step, b, kind).wait_recv()
+                if way == kind:
+                    ring_copy(way, step + 1, b, kind).start()
+                else:
+
+                    @pl.when(on)
+                    def _():
+                        ring_copy(way, step + 1, b, kind).start()
+
+    def last_wait(b):
+        for kind in range(2):
+            arrival(kind, HALF - 1, b, kind).wait_recv()
 
     scale = HD ** -0.5 * LOG2E
 
@@ -372,7 +376,7 @@
             block((z - HALF,), b, 0)
 
     def emit(b):
-        rows = jnp.transpose(out_acc[b] / total[b, 0:1])
+        rows = jnp.transpose(out_acc[b] * (1.0 / total[b, 0:1]))
         for h in range(SHARE):
             at = pl.ds(pl.multiple_of(b * (SHARE * HD), SHARE * HD) + h * HD, HD)
             o_ref[:, at] = jnp.where(
@@ -392,7 +396,7 @@
         xb(1, path, 5).start()
     kv_end(0)
     ring_begin(0)
-    relay(0, 0)
+    loop(0, FIRST, lambda b: relay(0, b))
 
     unit_s = (iota((SLOTS, nseq), 0) >> 5).astype(F32)
     group = g.astype(F32)
@@ -419,22 +423,21 @@
     )
     live[...] = jnp.broadcast_to(seq_s, (SLOTS, HD))
 
-    relay(1, 0)
-    relay(2, 0)
+    loop(0, FIRST, lambda b: relay(1, b))
     xb_wait(range(2, 6), 1)
     project(1)
     kv_begin(1)
-    relay(3, 0)
-    relay(4, 0)
+    loop(0, FIRST, lambda b: relay(2, b))
     kv_end(1)
     ring_begin(1)
+    loop(0, FIRST, lambda b: relay(3, b))
     loop(1, GROUPS, lambda k: q_copy(k).start())
     rq[g] = qp[g]
-    relay(5, 0)
-    relay(6, 0)
+    loop(0, FIRST, lambda b: relay(4, b))
     loop(FIRST, KVH, lambda b: relay(0, b))
-    arrival(0, HALF - 1, 0).wait_recv()
+    loop(0, FIRST, lambda b: relay(5, b))
     loop(FIRST, KVH, lambda b: relay(1, b))
+    loop(0, FIRST, lambda b: relay(6, b))
     q_take(1)
     arrived = rq[...].reshape(GROUPS * 16, q_cols)
     slot = iota((SLOTS, GROUPS * 16), 0)
@@ -460,37 +463,32 @@
 
         @pl.when(b == FIRST)
         def _():
-            attend(step, 0)
+            loop(0, FIRST, lambda c: attend(step, c))
 
     loop(2 * rest, (HALF - 1) * rest, steps)
-    loop(0, 2, lambda step: attend(step, 0))
-    attend_last(0)
-    emit(0)
+    loop(0, FIRST, lambda b: attend(0, b))
+    loop(0, FIRST, lambda b: attend(1, b))
+    for b in range(FIRST):
+        last_wait(b)
+        attend_last(b)
+    loop(0, FIRST, emit)
     loop(FIRST, KVH, lambda b: attend(HALF - 3, b))
     loop(FIRST, KVH, lambda b: attend(HALF - 2, b))
     for b in range(FIRST, KVH):
-        arrival(b % 2, HALF - 1, b).wait_recv()
+        last_wait(b)
         attend_last(b)
     loop(FIRST, KVH, emit)
 
     hid_copy.wait_send()
+    q_take(0)
     for part in range(2):
         wz_take(part, 0)
-        for path in range(2):
-            for k in range(3):
-                xa(part, path, k).wait_send()
-            for kind in range(3 if part == 0 else 6):
-                xb(part, path, kind).wait_send()
         kv_take(part, 0)
-    q_take(0)
-
-    def ring_sent(index):
-        ring_copy(0, index // KVH, lax.rem(index, KVH)).wait_send()
-        ring_copy(1, index // KVH, lax.rem(index, KVH)).wait_send()
-
-    loop(0, (HALF - 1) * KVH, ring_sent)
-    for b in range(KVH):
-        ring_copy(b % 2, HALF - 1, b).wait_send()
+        take(w.at[0:3, :, :, 0, :, cols(part)], xa_send.at[part])
+        take(w.at[0:3, :, :, :, :, cols(part)], xb_send.at[part])
+    for way in range(2):
+        take(buf.at[0 : HALF - 1], ring_send.at[way])
+        take(buf.at[0, :, 0], ring_send.at[way])
 
 
 def per_device(hidden, queries, key_weight, value_weight, lengths, assign):
@@ -525,12 +523,14 @@
             dma((2,)),
             dma((2,)),
             dma((2, 2)),
-            dma((2, 2, 2, 3)),
-            dma((2, 2, 2, 6)),
+            dma((2,)),
+            dma((2, 2, 3)),
+            dma((2,)),
+            dma((2, 2, 6)),
             dma((2, 2)),
             dma((2,)),
-            dma((2, HALF, KVH)),
-            dma((2, HALF, KVH)),
+            dma((2,)),
+            dma((2, HALF, KVH, 2)),
         ],
         compiler_params=pltpu.CompilerParams(
             collective_id=0, has_side_effects=True, vmem_limit_bytes=VMEM_BYTES

time: 140 us -> 134 us (0.957)
  Pallas kernels: 137 us -> 132 us
    pallas_call x1, Pallas kernels: 137 us -> 132 us  [per_device(): pl.pallas_call(kernel, out_shape=jax.ShapeDtypeStruct((SLOTS, H * HD), BF...]
where the time goes in v4:
time: 134 us
  Pallas kernels  132 us (99%)
  local copies, waits for them, and re-layouts  2.09 us (2%)
    pallas_call x1, Pallas kernels, per_device(): pl.pallas_call(kernel, out_shape=jax.ShapeDtypeStruct((SLOTS, H * HD), BF...  132 us

profile of v4, /device:TPU:6, one launch (start us, length us, event | category | flops | bytes accessed | tf_op | source)
XLA Modules:
  0.0 133.8 jit_solution(17820238711131621837)
XLA Ops:
  0.0 131.7 %attend.1 = bf16[192,2048]{1,0:T(8,128)(2,1)} custom-call(bf16[128,4096]{1,0:T(8,128)(2,1)} %bitcast.6, bf16[128,2048]{1,0:T(8,128)(2,1)} %bitcast.7, bf16[256,512]{1,0:T(8,128)(2,1)} %wk_ref.1, bf16[256,512]{1,0:T(8,128)(2,1)} %wv_ref.1, s32[1,64]{1,0:T(1,128)} %bitcast.8, s32[1,64]{1,0:T(1,128)} %bitcast.9, f32[1,128]{1,0:T(1,128)} %constant.2.clone.freq_ref), custom_call_target="tpu_custom_call" | custom-call | tf_op jit(solution)/shard_map/attend/pallas_call | solution.py:500
  131.7 2.1 %copy.9 = bf16[1,192,2048]{2,1,0:T(8,128)(2,1)} copy(bf16[1,192,2048]{2,1,0:T(8,128)(2,1)} %bitcast.5) | data formatting | bytes 1572864

commit v5 on v4

--- a/solution.py
+++ b/solution.py
@@ -134,18 +134,15 @@
         place = (y, x)[path]
         peer = (y_peer, x_peer)[path]
         low = 2 * path
-        both, one, two = slice(low, low + 2), slice(low, low + 1), slice(low + 1, low + 2)
-        if part == 0:
-            slab, device = xb_view(part, path, both, place), peer((2, 1, 3)[kind])
-        else:
-            slab, device = (
-                (xb_view(part, path, one, place), peer(1)),
-                (xb_view(part, path, two, place), peer(3)),
-                (xb_view(part, path, two, place), peer(1)),
-                (xb_view(part, path, one, place), peer(3)),
-                (xb_view(part, path, one, lax.rem(place + 3, 4)), peer(1)),
-                (xb_view(part, path, two, lax.rem(place + 1, 4)), peer(3)),
-            )[kind]
+        one, two = slice(low, low + 1), slice(low + 1, low + 2)
+        slab, device = (
+            (xb_view(part, path, one, place), peer(1)),
+            (xb_view(part, path, two, place), peer(3)),
+            (xb_view(part, path, two, place), peer(1)),
+            (xb_view(part, path, one, place), peer(3)),
+            (xb_view(part, path, one, lax.rem(place + 3, 4)), peer(1)),
+            (xb_view(part, path, two, lax.rem(place + 1, 4)), peer(3)),
+        )[kind]
         return rdma(
             slab, slab, xb_send.at[part], xb_sem.at[part, path, kind], device
         )
@@ -159,6 +156,13 @@
         for path in range(2):
             for kind in kinds:
                 xb(part, path, kind).wait_recv()
+
+    def xb_relay(part):
+        for path in range(2):
+            xb(part, path, 0).wait_recv()
+            xb(part, path, 4).start()
+            xb(part, path, 1).wait_recv()
+            xb(part, path, 5).start()
 
     def xa_start(part):
         for path in range(2):
@@ -208,9 +212,9 @@
         cos[at, :] = cosine
         sin[at, :] = jnp.where(iota((ROWS, HD), 1) < HD // 2, -sine, sine)
     wz_take(1, 1)
+    xa_start(1)
     xa_wait(0)
-    xb_start(range(3), 0)
-    xa_start(1)
+    xb_start(range(4), 0)
 
     q_in.wait()
     q_cols = H * HD // 2
@@ -383,17 +387,14 @@
                 live[...] > 0.5, rows[h * SLOTS : (h + 1) * SLOTS], 0.0
             ).astype(BF16)
 
+    xb_relay(0)
     xa_wait(1)
-    xb_wait(range(3), 0)
     xb_start(range(4), 1)
+    xb_wait(range(2, 6), 0)
     hid_copy.wait_recv()
     project(0)
     kv_begin(0)
-    for path in range(2):
-        xb(1, path, 0).wait_recv()
-        xb(1, path, 4).start()
-        xb(1, path, 1).wait_recv()
-        xb(1, path, 5).start()
+    xb_relay(1)
     kv_end(0)
     ring_begin(0)
     loop(0, FIRST, lambda b: relay(0, b))
@@ -423,10 +424,10 @@
     )
     live[...] = jnp.broadcast_to(seq_s, (SLOTS, HD))
 
-    loop(0, FIRST, lambda b: relay(1, b))
     xb_wait(range(2, 6), 1)
     project(1)
     kv_begin(1)
+    loop(0, FIRST, lambda b: relay(1, b))
     loop(0, FIRST, lambda b: relay(2, b))
     kv_end(1)
     ring_begin(1)

time: 134 us -> 129 us (0.963)
  Pallas kernels: 132 us -> 126 us
    pallas_call x1, Pallas kernels: 132 us -> 126 us  [per_device(): pl.pallas_call(kernel, out_shape=jax.ShapeDtypeStruct((SLOTS, H * HD), BF...]
where the time goes in v5:
time: 129 us; the launch traced here: 128 us
  Pallas kernels  126 us (98%)
  local copies, waits for them, and re-layouts  2.09 us (2%)
    pallas_call x1, Pallas kernels, per_device(): pl.pallas_call(kernel, out_shape=jax.ShapeDtypeStruct((SLOTS, H * HD), BF...  126 us

profile of v5, /device:TPU:6, one launch (start us, length us, event | category | flops | bytes accessed | tf_op | source)
XLA Modules:
  0.0 128.1 jit_solution(5920091975877961484)
XLA Ops:
  0.0 126.0 %attend.1 = bf16[192,2048]{1,0:T(8,128)(2,1)} custom-call(bf16[128,4096]{1,0:T(8,128)(2,1)} %bitcast.6, bf16[128,2048]{1,0:T(8,128)(2,1)} %bitcast.7, bf16[256,512]{1,0:T(8,128)(2,1)} %wk_ref.1, bf16[256,512]{1,0:T(8,128)(2,1)} %wv_ref.1, s32[1,64]{1,0:T(1,128)} %bitcast.8, s32[1,64]{1,0:T(1,128)} %bitcast.9, f32[1,128]{1,0:T(1,128)} %constant.2.clone.freq_ref), custom_call_target="tpu_custom_call" | custom-call | tf_op jit(solution)/shard_map/attend/pallas_call | solution.py:501
  126.0 2.1 %copy.9 = bf16[1,192,2048]{2,1,0:T(8,128)(2,1)} copy(bf16[1,192,2048]{2,1,0:T(8,128)(2,1)} %bitcast.5) | data formatting | bytes 1572864

commit v6 on v5

--- a/solution.py
+++ b/solution.py
@@ -394,9 +394,9 @@
     hid_copy.wait_recv()
     project(0)
     kv_begin(0)
-    xb_relay(1)
     kv_end(0)
     ring_begin(0)
+    xb_relay(1)
     loop(0, FIRST, lambda b: relay(0, b))
 
     unit_s = (iota((SLOTS, nseq), 0) >> 5).astype(F32)

time: 129 us -> 128 us (level)
  no operation moved by 1% of the time
where the time goes in v6:
time: 128 us; the launch traced here: 127 us
  Pallas kernels  125 us (98%)
  local copies, waits for them, and re-layouts  2.09 us (2%)
    pallas_call x1, Pallas kernels, per_device(): pl.pallas_call(kernel, out_shape=jax.ShapeDtypeStruct((SLOTS, H * HD), BF...  125 us

profile of v6, /device:TPU:6, one launch (start us, length us, event | category | flops | bytes accessed | tf_op | source)
XLA Modules:
  0.0 127.5 jit_solution(1092828703596181214)
XLA Ops:
  0.0 125.4 %attend.1 = bf16[192,2048]{1,0:T(8,128)(2,1)} custom-call(bf16[128,4096]{1,0:T(8,128)(2,1)} %bitcast.6, bf16[128,2048]{1,0:T(8,128)(2,1)} %bitcast.7, bf16[256,512]{1,0:T(8,128)(2,1)} %wk_ref.1, bf16[256,512]{1,0:T(8,128)(2,1)} %wv_ref.1, s32[1,64]{1,0:T(1,128)} %bitcast.8, s32[1,64]{1,0:T(1,128)} %bitcast.9, f32[1,128]{1,0:T(1,128)} %constant.2.clone.freq_ref), custom_call_target="tpu_custom_call" | custom-call | tf_op jit(solution)/shard_map/attend/pallas_call | solution.py:501
  125.4 2.1 %copy.9 = bf16[1,192,2048]{2,1,0:T(8,128)(2,1)} copy(bf16[1,192,2048]{2,1,0:T(8,128)(2,1)} %bitcast.5) | data formatting | bytes 1572864
